TPU v7x, 128 devices: a whole 4x4x4 slice. The times are simulated.
128 devices in a mesh: ctx: 16 (over z_hi, y, core), heads: 8 (over z_lo, x).
Axes of the slice: x: 4, y: 4, z: 4 (z_hi: 2, z_lo: 2; z = z_hi * 2 + z_lo), core: 2. Of those that a mesh axis runs over, the one named last changes fastest.
Arguments:
- stretch_order: int32 [32], replicated, may hold values from 0 to 31, as said below
- query_heads: bfloat16 [2048, 4096], P('ctx', 'heads'), may hold values from -5 to 5
- key_heads: bfloat16 [2048, 4096], P('ctx', 'heads'), may hold values from -5 to 5
- value_heads: bfloat16 [2048, 4096], P('ctx', 'heads'), may hold values from -6 to 6
- output_grad: bfloat16 [2048, 4096], P('ctx', 'heads'), may hold values from -6 to 6
- query_weight: bfloat16 [4096, 4096], P(None, 'heads'), may hold values from -0.09375 to 0.09375
- key_weight: bfloat16 [4096, 4096], P(None, 'heads'), may hold values from -0.09375 to 0.09375
- value_weight: bfloat16 [4096, 4096], P(None, 'heads'), may hold values from -0.09375 to 0.09375
- output_weight: bfloat16 [4096, 4096], P('heads'), may hold values from -0.09375 to 0.09375
- head_lambda: float32 [16], P('heads'), may hold values from 0.2 to 0.8
- norm_gain: float32 [256], replicated, may hold values from 0.1 to 1.9
Outputs:
- input_grad: float32 [4096, 2048], P('heads', 'ctx')
Inputs may be any that keep to these rules, and one draw needn't show every extreme that they name: `stretch_order`: every stretch 0 to 31 appears once; entries 2 d and 2 d + 1 always sum to 31.
All inputs are finite; a program needn't handle non-finite values.
Results may differ from a plain program's by a relative error of at most 0.024.
Values may be sent and summed in bfloat16 or wider, within the bound.
A program may use at most 128 MiB of HBM per device.

v0:
```python
import jax
import jax.numpy as jnp
from jax import lax
from jax.sharding import PartitionSpec as P

HDIM = 128


lambda_init = 0.8
norm_epsilon = 1e-05
mask_value = -1e30


def shifted(value, axis, steps):
    count = lax.axis_size(axis)
    pairs = [(source, (source + steps) % count) for source in range(count)]
    return lax.ppermute(value, axis, pairs)


def block_positions(stretch_order, block_index, length):
    stretch_pair = lax.dynamic_slice_in_dim(stretch_order, 2 * block_index, 2, 0)
    within = length // 2
    row_index = jnp.arange(length, dtype=jnp.int32)
    return (
        jnp.where(row_index < within, stretch_pair[0], stretch_pair[1]) * within
        + row_index % within
    )


def body(
    stretch_order,
    query_heads,
    key_heads,
    value_heads,
    output_grad,
    query_weight,
    key_weight,
    value_weight,
    output_weight,
    head_lambda,
    norm_gain,
):
    length = query_heads.shape[0]
    heads_here = head_lambda.shape[0]
    head_width = 2 * HDIM
    score_scale = HDIM ** (-0.5)
    devices = lax.axis_size("ctx")
    own_block = lax.axis_index("ctx")
    query_positions = block_positions(stretch_order, own_block, length)
    query_four = query_heads.reshape(length, heads_here, 2, HDIM)
    second_weight = head_lambda[:, None, None]
    map_weight = jnp.stack([jnp.ones_like(head_lambda), -head_lambda])[:, :, None, None]
    out_heads = lax.dot_general(
        lax.all_gather(output_grad, "heads", axis=1, tiled=True),
        output_weight,
        (((1,), (1,)), ((), ())),
        preferred_element_type=jnp.float32,
    )

    def masked_scores(key_four, key_positions):
        visible = key_positions[None, :] <= query_positions[:, None]
        scores = (
            jnp.einsum("qhmd,khmd->mhqk", query_four, key_four, preferred_element_type=jnp.float32)
            * score_scale
        )
        return (scores, visible)

    def stats_step(carried, key_value, key_positions):
        row_peak, running = carried
        key_four = key_value[0].reshape(length, heads_here, 2, HDIM)
        scores, visible = masked_scores(key_four, key_positions)
        new_peak = jnp.maximum(row_peak, jnp.max(jnp.where(visible, scores, mask_value), axis=-1))
        weights = jnp.where(visible, jnp.exp(scores - new_peak[..., None]), 0.0)
        running = running * jnp.exp(row_peak - new_peak) + jnp.sum(weights, axis=-1)
        return (new_peak, running)

    def values_maker(log_total):

        def values_step(weighted, key_value, key_positions):
            key_four = key_value[0].reshape(length, heads_here, 2, HDIM)
            value_three = key_value[1].reshape(length, heads_here, head_width)
            scores, visible = masked_scores(key_four, key_positions)
            probabilities = jnp.where(visible, jnp.exp(scores - log_total[..., None]), 0.0).astype(
                jnp.bfloat16
            )
            return weighted + jnp.einsum(
                "mhqk,khe->mhqe", probabilities, value_three, preferred_element_type=jnp.float32
            )

        return values_step

    def backward_core(
        query_side,
        log_total,
        grad_attn,
        row_stats,
        side_positions,
        key_block,
        value_block,
        key_positions,
    ):
        key_four = key_block.reshape(length, heads_here, 2, HDIM)
        value_three = value_block.reshape(length, heads_here, head_width)
        visible = key_positions[None, :] <= side_positions[:, None]
        scores = (
            jnp.einsum("qhmd,khmd->mhqk", query_side, key_four, preferred_element_type=jnp.float32)
            * score_scale
        )
        probabilities = jnp.where(visible, jnp.exp(scores - log_total[..., None]), 0.0)
        grad_weights = jnp.einsum(
            "hqe,khe->hqk", grad_attn, value_three, preferred_element_type=jnp.float32
        )
        score_grad = (
            map_weight * probabilities * (grad_weights[None] - row_stats[..., None])
        ).astype(jnp.bfloat16)
        mixed_weights = (probabilities[0] - second_weight * probabilities[1]).astype(jnp.bfloat16)
        value_grad = jnp.einsum(
            "hqk,hqe->khe", mixed_weights, grad_attn, preferred_element_type=jnp.float32
        )
        query_delta = score_scale * jnp.einsum(
            "mhqk,khmd->qhmd", score_grad, key_four, preferred_element_type=jnp.float32
        )
        key_grad = score_scale * jnp.einsum(
            "mhqk,qhmd->khmd", score_grad, query_side, preferred_element_type=jnp.float32
        )
        return (
            query_delta,
            key_grad.reshape(length, heads_here * head_width),
            value_grad.reshape(length, heads_here * head_width),
        )

    def backward_step(prepared, query_grad, key_block, value_block, key_positions):
        log_total, grad_attn, row_stats = prepared
        query_delta, key_grad, value_grad = backward_core(
            query_four,
            log_total,
            grad_attn,
            row_stats,
            query_positions,
            key_block,
            value_block,
            key_positions,
        )
        return (query_grad + query_delta, key_grad, value_grad)

    stats_start = (
        jnp.full((2, heads_here, length), mask_value, jnp.float32),
        jnp.zeros((2, heads_here, length), jnp.float32),
    )
    values_start = jnp.zeros((2, heads_here, length, head_width), jnp.float32)
    query_start = jnp.zeros((length, heads_here, 2, HDIM), jnp.float32)
    grad_shape = (length, heads_here * head_width)
    last_source = (own_block + 1) % devices

    def key_cycle(step_fn, initial):

        def advance(cycle_step, forward_carry):
            carried, key_value = forward_carry
            source = (own_block - cycle_step) % devices
            carried = step_fn(carried, key_value, block_positions(stretch_order, source, length))
            key_value = shifted((key_value[0], key_value[1]), "ctx", 1)
            return (carried, key_value)

        carried, key_value = lax.fori_loop(
            0, devices - 1, advance, (initial, (key_heads, value_heads))
        )
        return step_fn(carried, key_value, block_positions(stretch_order, last_source, length))

    row_peak, running = key_cycle(stats_step, stats_start)
    log_total = row_peak + jnp.log(running)
    outputs = key_cycle(values_maker(log_total), values_start)
    combined = outputs[0] - second_weight * outputs[1]
    root_mean = jnp.sqrt(jnp.mean(combined * combined, axis=-1, keepdims=True) + norm_epsilon)
    normed = combined / root_mean
    grad_normed = (
        jnp.transpose(out_heads.reshape(length, heads_here, head_width), (1, 0, 2))
        * norm_gain
        * (1.0 - lambda_init)
    )
    grad_attn = (
        (grad_normed - normed * jnp.mean(grad_normed * normed, axis=-1, keepdims=True)) / root_mean
    ).astype(jnp.bfloat16)
    row_stats = jnp.sum(grad_attn.astype(jnp.float32)[None] * outputs, axis=-1)
    prepared = (log_total, grad_attn, row_stats)

    def send_home(grad_sums):
        return shifted((grad_sums[0], grad_sums[1]), "ctx", 1)

    def backward_cycle(cycle_step, backward_carry):
        query_grad, key_value, grad_sums = backward_carry
        source = (own_block - cycle_step) % devices
        query_grad, key_grad, value_grad = backward_step(
            prepared,
            query_grad,
            key_value[0],
            key_value[1],
            block_positions(stretch_order, source, length),
        )
        grad_sums = send_home((grad_sums[0] + key_grad, grad_sums[1] + value_grad))
        key_value = shifted((key_value[0], key_value[1]), "ctx", 1)
        return (query_grad, key_value, grad_sums)

    empty_sums = (jnp.zeros(grad_shape, jnp.float32), jnp.zeros(grad_shape, jnp.float32))
    query_grad, key_value, grad_sums = lax.fori_loop(
        0, devices - 1, backward_cycle, (query_start, (key_heads, value_heads), empty_sums)
    )
    query_grad, key_grad, value_grad = backward_step(
        prepared,
        query_grad,
        key_value[0],
        key_value[1],
        block_positions(stretch_order, last_source, length),
    )
    key_total, value_total = send_home((grad_sums[0] + key_grad, grad_sums[1] + value_grad))
    query_flat = query_grad.reshape(grad_shape).astype(jnp.bfloat16)
    key_flat = key_total.astype(jnp.bfloat16)
    value_flat = value_total.astype(jnp.bfloat16)
    running = jnp.zeros(
        (query_weight.shape[0] // lax.axis_size("heads") * lax.axis_size("heads"), length),
        jnp.float32,
    )
    for gradient, projection in (
        (query_flat, query_weight),
        (key_flat, key_weight),
        (value_flat, value_weight),
    ):
        running = running + lax.dot_general(
            projection, gradient, (((1,), (1,)), ((), ())), preferred_element_type=jnp.float32
        )
    return lax.psum_scatter(running, "heads", scatter_dimension=0, tiled=True)


def solution(mesh):
    in_specs = (
        P(),
        P("ctx", "heads"),
        P("ctx", "heads"),
        P("ctx", "heads"),
        P("ctx", "heads"),
        P(None, "heads"),
        P(None, "heads"),
        P(None, "heads"),
        P("heads", None),
        P("heads"),
        P(),
    )
    out_specs = P("heads", "ctx")
    return jax.shard_map(body, mesh=mesh, in_specs=in_specs, out_specs=out_specs, check_vma=False)
```

profile of v0, /device:TPU:0, one launch (start us, length us, event | category | flops | bytes accessed | tf_op | source)
XLA Modules:
  0.0 641.7 jit_solution(5168965759900095650)
XLA Ops:
  12.6 123.8 %while.67 = (s32[]{:T(128)}, f32[2,2,128]{2,1,0:T(2,128)S(1)}, f32[2,2,128]{2,1,0:T(2,128)S(1)}, bf16[128,512]{1,0:T(8,128)(2,1)S(1)}, s32[]{:T(128)}, /*index=5...) while((s32[]{:T(128)}, f32[2,2,128]{2,1,0:T(2,128)S(1)}, ...), condition=%wide.region_3.4_spmd.clone, body=%wide.region_0.3_spmd.clone.sunk | while | flops 17191952 | bytes 1913243 | solution.py:164
  17.0 4.2 collective-permute-done
  25.6 4.4 collective-permute-done
  34.4 4.0 collective-permute-done
  42.9 4.5 collective-permute-done
  51.8 3.7 collective-permute-done
  59.9 3.7 collective-permute-done
  68.0 3.7 collective-permute-done
  76.1 3.7 collective-permute-done
  84.2 3.7 collective-permute-done
  92.3 3.7 collective-permute-done
  100.4 3.7 collective-permute-done
  108.5 3.7 collective-permute-done
  116.6 3.7 collective-permute-done
  124.6 3.7 collective-permute-done
  132.7 3.7 collective-permute-done
  138.2 142.4 %while.68 = (s32[]{:T(128)}, f32[2,2,128,256]{3,2,0,1:T(8,128)S(1)}, bf16[128,512]{1,0:T(8,128)(2,1)S(1)}, bf16[128,512]{1,0:T(8,128)(2,1)S(1)}, s32[]{:T(128)},...) while((s32[]{:T(128)}, ...), condition=%wide.region_7.8_spmd.clone, body=%wide.region_6.7_spmd.clone.sunk | while | flops 50874896 | bytes 3576266 | solution.py:164
  142.9 3.3 collective-permute-done.1
  152.4 3.3 collective-permute-done.1
  161.9 3.3 collective-permute-done.1
  171.4 3.3 collective-permute-done.1
  180.9 3.3 collective-permute-done.1
  190.4 3.3 collective-permute-done.1
  199.9 3.3 collective-permute-done.1
  218.9 3.3 collective-permute-done.1
  247.3 3.3 collective-permute-done.1
  266.3 3.3 collective-permute-done.1
  275.8 3.3 collective-permute-done.1
  281.6 3.8 fusion.107
  285.9 290.8 %while.69 = (s32[]{:T(128)}, f32[128,2,2,128]{3,0,2,1:T(8,128)S(1)}, bf16[128,512]{1,0:T(8,128)(2,1)S(1)}, bf16[128,512]{1,0:T(8,128)(2,1)S(1)}, f32[128,512]{0,...) while((s32[]{:T(128)}, ...), condition=%wide.region_12.13_spmd.clone, body=%wide.region_11.12_spmd.clone.sunk | while | flops 84855296 | bytes 9738850 | solution.py:204
  291.2 12.7 %collective-permute-done.3 = bf16[128,512]{1,0:T(8,128)(2,1)S(1)} collective-permute-done((bf16[128,512]{1,0:T(8,128)(2,1)S(1)}, bf16[128,512]{1,0:T(8,128)(2,1)S(1)}, u32[]{:S(2)}, u32[]{:S(2)}) %collective-permute-start.3) | collective-permute-done | bytes 131104 | tf_op jit(solution)/shard_map/while/body/eval_jaxpr/ppermute | solution.py:17
  310.6 12.7 %collective-permute-done.3 = bf16[128,512]{1,0:T(8,128)(2,1)S(1)} collective-permute-done((bf16[128,512]{1,0:T(8,128)(2,1)S(1)}, bf16[128,512]{1,0:T(8,128)(2,1)S(1)}, u32[]{:S(2)}, u32[]{:S(2)}) %collective-permute-start.3) | collective-permute-done | bytes 131104 | tf_op jit(solution)/shard_map/while/body/eval_jaxpr/ppermute | solution.py:17
  330.0 12.7 %collective-permute-done.3 = bf16[128,512]{1,0:T(8,128)(2,1)S(1)} collective-permute-done((bf16[128,512]{1,0:T(8,128)(2,1)S(1)}, bf16[128,512]{1,0:T(8,128)(2,1)S(1)}, u32[]{:S(2)}, u32[]{:S(2)}) %collective-permute-start.3) | collective-permute-done | bytes 131104 | tf_op jit(solution)/shard_map/while/body/eval_jaxpr/ppermute | solution.py:17
  349.4 12.7 %collective-permute-done.3 = bf16[128,512]{1,0:T(8,128)(2,1)S(1)} collective-permute-done((bf16[128,512]{1,0:T(8,128)(2,1)S(1)}, bf16[128,512]{1,0:T(8,128)(2,1)S(1)}, u32[]{:S(2)}, u32[]{:S(2)}) %collective-permute-start.3) | collective-permute-done | bytes 131104 | tf_op jit(solution)/shard_map/while/body/eval_jaxpr/ppermute | solution.py:17
  368.8 12.7 %collective-permute-done.3 = bf16[128,512]{1,0:T(8,128)(2,1)S(1)} collective-permute-done((bf16[128,512]{1,0:T(8,128)(2,1)S(1)}, bf16[128,512]{1,0:T(8,128)(2,1)S(1)}, u32[]{:S(2)}, u32[]{:S(2)}) %collective-permute-start.3) | collective-permute-done | bytes 131104 | tf_op jit(solution)/shard_map/while/body/eval_jaxpr/ppermute | solution.py:17
  388.2 12.7 %collective-permute-done.3 = bf16[128,512]{1,0:T(8,128)(2,1)S(1)} collective-permute-done((bf16[128,512]{1,0:T(8,128)(2,1)S(1)}, bf16[128,512]{1,0:T(8,128)(2,1)S(1)}, u32[]{:S(2)}, u32[]{:S(2)}) %collective-permute-start.3) | collective-permute-done | bytes 131104 | tf_op jit(solution)/shard_map/while/body/eval_jaxpr/ppermute | solution.py:17
  407.5 12.7 %collective-permute-done.3 = bf16[128,512]{1,0:T(8,128)(2,1)S(1)} collective-permute-done((bf16[128,512]{1,0:T(8,128)(2,1)S(1)}, bf16[128,512]{1,0:T(8,128)(2,1)S(1)}, u32[]{:S(2)}, u32[]{:S(2)}) %collective-permute-start.3) | collective-permute-done | bytes 131104 | tf_op jit(solution)/shard_map/while/body/eval_jaxpr/ppermute | solution.py:17
  426.9 12.7 %collective-permute-done.3 = bf16[128,512]{1,0:T(8,128)(2,1)S(1)} collective-permute-done((bf16[128,512]{1,0:T(8,128)(2,1)S(1)}, bf16[128,512]{1,0:T(8,128)(2,1)S(1)}, u32[]{:S(2)}, u32[]{:S(2)}) %collective-permute-start.3) | collective-permute-done | bytes 131104 | tf_op jit(solution)/shard_map/while/body/eval_jaxpr/ppermute | solution.py:17
  446.3 12.7 %collective-permute-done.3 = bf16[128,512]{1,0:T(8,128)(2,1)S(1)} collective-permute-done((bf16[128,512]{1,0:T(8,128)(2,1)S(1)}, bf16[128,512]{1,0:T(8,128)(2,1)S(1)}, u32[]{:S(2)}, u32[]{:S(2)}) %collective-permute-start.3) | collective-permute-done | bytes 131104 | tf_op jit(solution)/shard_map/while/body/eval_jaxpr/ppermute | solution.py:17
  465.7 12.7 %collective-permute-done.3 = bf16[128,512]{1,0:T(8,128)(2,1)S(1)} collective-permute-done((bf16[128,512]{1,0:T(8,128)(2,1)S(1)}, bf16[128,512]{1,0:T(8,128)(2,1)S(1)}, u32[]{:S(2)}, u32[]{:S(2)}) %collective-permute-start.3) | collective-permute-done | bytes 131104 | tf_op jit(solution)/shard_map/while/body/eval_jaxpr/ppermute | solution.py:17
  485.1 12.7 %collective-permute-done.3 = bf16[128,512]{1,0:T(8,128)(2,1)S(1)} collective-permute-done((bf16[128,512]{1,0:T(8,128)(2,1)S(1)}, bf16[128,512]{1,0:T(8,128)(2,1)S(1)}, u32[]{:S(2)}, u32[]{:S(2)}) %collective-permute-start.3) | collective-permute-done | bytes 131104 | tf_op jit(solution)/shard_map/while/body/eval_jaxpr/ppermute | solution.py:17
  504.5 12.7 %collective-permute-done.3 = bf16[128,512]{1,0:T(8,128)(2,1)S(1)} collective-permute-done((bf16[128,512]{1,0:T(8,128)(2,1)S(1)}, bf16[128,512]{1,0:T(8,128)(2,1)S(1)}, u32[]{:S(2)}, u32[]{:S(2)}) %collective-permute-start.3) | collective-permute-done | bytes 131104 | tf_op jit(solution)/shard_map/while/body/eval_jaxpr/ppermute | solution.py:17
  523.9 12.7 %collective-permute-done.3 = bf16[128,512]{1,0:T(8,128)(2,1)S(1)} collective-permute-done((bf16[128,512]{1,0:T(8,128)(2,1)S(1)}, bf16[128,512]{1,0:T(8,128)(2,1)S(1)}, u32[]{:S(2)}, u32[]{:S(2)}) %collective-permute-start.3) | collective-permute-done | bytes 131104 | tf_op jit(solution)/shard_map/while/body/eval_jaxpr/ppermute | solution.py:17
  543.2 12.7 %collective-permute-done.3 = bf16[128,512]{1,0:T(8,128)(2,1)S(1)} collective-permute-done((bf16[128,512]{1,0:T(8,128)(2,1)S(1)}, bf16[128,512]{1,0:T(8,128)(2,1)S(1)}, u32[]{:S(2)}, u32[]{:S(2)}) %collective-permute-start.3) | collective-permute-done | bytes 131104 | tf_op jit(solution)/shard_map/while/body/eval_jaxpr/ppermute | solution.py:17
  562.6 12.7 %collective-permute-done.3 = bf16[128,512]{1,0:T(8,128)(2,1)S(1)} collective-permute-done((bf16[128,512]{1,0:T(8,128)(2,1)S(1)}, bf16[128,512]{1,0:T(8,128)(2,1)S(1)}, u32[]{:S(2)}, u32[]{:S(2)}) %collective-permute-start.3) | collective-permute-done | bytes 131104 | tf_op jit(solution)/shard_map/while/body/eval_jaxpr/ppermute | solution.py:17
  578.6 3.8 fusion.108
  582.5 4.5 collective-permute-done.7
  591.3 41.7 %reduce-scatter.2.cloned.1.call-done = f32[512,128]{0,1:T(8,128)} async-done(((f32[4096,128]{0,1:T(8,128)}), f32[512,128]{0,1:T(8,128)}) %reduce-scatter.2.cloned.1.call-update) | async-done | bytes 262160 | tf_op jit(solution)/shard_map/reduce_scatter | solution.py:230
  (825 shorter events, 284.7 us)
Async XLA Ops:
  6.5 275.1 %all-gather.2.cloned.1.call-start = ((), (), s32[]{:S(2)}) async-start(), calls=%async_computation.1 | async-start | bytes 1179648 | tf_op jit(solution)/shard_map/all_gather | solution.py:54
  8.4 624.7 %reduce-scatter.2.cloned.1.call-start = ((), (), s32[]{:S(2)}) async-start(), calls=%async_computation.2 | async-start | bytes 2359296 | tf_op jit(solution)/shard_map/reduce_scatter | solution.py:230
  290.2 15.1 %collective-permute-start.5 = (f32[128,512]{0,1:T(8,128)S(1)}, f32[128,512]{0,1:T(8,128)S(1)}, u32[]{:S(2)}, u32[]{:S(2)}) collective-permute-start(f32[128,512]{0,1:T(8,128)S(1)} %bitcast_add_fusion.6), channel_id=1, source_target_pairs={{0,8},{8,16},{16,24},{24,32},{32,40},{40,48},{48,56},{56,64},{64,7... | collective-permute-start | bytes 786440 | tf_op jit(solution)/shard_map/while/body/eval_jaxpr/ppermute | solution.py:17
  290.8 14.6 %collective-permute-start.6 = (f32[128,512]{0,1:T(8,128)S(1)}, f32[128,512]{0,1:T(8,128)S(1)}, u32[]{:S(2)}, u32[]{:S(2)}) collective-permute-start(f32[128,512]{0,1:T(8,128)S(1)} %bitcast_add_fusion.7), channel_id=1, source_target_pairs={{0,8},{8,16},{16,24},{24,32},{32,40},{40,48},{48,56},{56,64},{64,7... | collective-permute-start | bytes 786440 | tf_op jit(solution)/shard_map/while/body/eval_jaxpr/ppermute | solution.py:17
  290.9 14.4 %collective-permute-start.4 = (bf16[128,512]{1,0:T(8,128)(2,1)S(1)}, bf16[128,512]{1,0:T(8,128)(2,1)S(1)}, u32[]{:S(2)}, u32[]{:S(2)}) collective-permute-start(bf16[128,512]{1,0:T(8,128)(2,1)S(1)} %copy.259), channel_id=1, source_target_pairs={{0,8},{8,16},{16,24},{24,32},{32,40},{40,48},{48,56},{56,64},{64,7... | collective-permute-start | bytes 393224 | tf_op jit(solution)/shard_map/while/body/eval_jaxpr/ppermute | solution.py:17
  309.6 15.1 %collective-permute-start.5 = (f32[128,512]{0,1:T(8,128)S(1)}, f32[128,512]{0,1:T(8,128)S(1)}, u32[]{:S(2)}, u32[]{:S(2)}) collective-permute-start(f32[128,512]{0,1:T(8,128)S(1)} %bitcast_add_fusion.6), channel_id=1, source_target_pairs={{0,8},{8,16},{16,24},{24,32},{32,40},{40,48},{48,56},{56,64},{64,7... | collective-permute-start | bytes 786440 | tf_op jit(solution)/shard_map/while/body/eval_jaxpr/ppermute | solution.py:17
  310.2 14.6 %collective-permute-start.6 = (f32[128,512]{0,1:T(8,128)S(1)}, f32[128,512]{0,1:T(8,128)S(1)}, u32[]{:S(2)}, u32[]{:S(2)}) collective-permute-start(f32[128,512]{0,1:T(8,128)S(1)} %bitcast_add_fusion.7), channel_id=1, source_target_pairs={{0,8},{8,16},{16,24},{24,32},{32,40},{40,48},{48,56},{56,64},{64,7... | collective-permute-start | bytes 786440 | tf_op jit(solution)/shard_map/while/body/eval_jaxpr/ppermute | solution.py:17
  310.3 14.4 %collective-permute-start.4 = (bf16[128,512]{1,0:T(8,128)(2,1)S(1)}, bf16[128,512]{1,0:T(8,128)(2,1)S(1)}, u32[]{:S(2)}, u32[]{:S(2)}) collective-permute-start(bf16[128,512]{1,0:T(8,128)(2,1)S(1)} %copy.259), channel_id=1, source_target_pairs={{0,8},{8,16},{16,24},{24,32},{32,40},{40,48},{48,56},{56,64},{64,7... | collective-permute-start | bytes 393224 | tf_op jit(solution)/shard_map/while/body/eval_jaxpr/ppermute | solution.py:17
  329.0 15.1 %collective-permute-start.5 = (f32[128,512]{0,1:T(8,128)S(1)}, f32[128,512]{0,1:T(8,128)S(1)}, u32[]{:S(2)}, u32[]{:S(2)}) collective-permute-start(f32[128,512]{0,1:T(8,128)S(1)} %bitcast_add_fusion.6), channel_id=1, source_target_pairs={{0,8},{8,16},{16,24},{24,32},{32,40},{40,48},{48,56},{56,64},{64,7... | collective-permute-start | bytes 786440 | tf_op jit(solution)/shard_map/while/body/eval_jaxpr/ppermute | solution.py:17
  329.5 14.6 %collective-permute-start.6 = (f32[128,512]{0,1:T(8,128)S(1)}, f32[128,512]{0,1:T(8,128)S(1)}, u32[]{:S(2)}, u32[]{:S(2)}) collective-permute-start(f32[128,512]{0,1:T(8,128)S(1)} %bitcast_add_fusion.7), channel_id=1, source_target_pairs={{0,8},{8,16},{16,24},{24,32},{32,40},{40,48},{48,56},{56,64},{64,7... | collective-permute-start | bytes 786440 | tf_op jit(solution)/shard_map/while/body/eval_jaxpr/ppermute | solution.py:17
  329.7 14.4 %collective-permute-start.4 = (bf16[128,512]{1,0:T(8,128)(2,1)S(1)}, bf16[128,512]{1,0:T(8,128)(2,1)S(1)}, u32[]{:S(2)}, u32[]{:S(2)}) collective-permute-start(bf16[128,512]{1,0:T(8,128)(2,1)S(1)} %copy.259), channel_id=1, source_target_pairs={{0,8},{8,16},{16,24},{24,32},{32,40},{40,48},{48,56},{56,64},{64,7... | collective-permute-start | bytes 393224 | tf_op jit(solution)/shard_map/while/body/eval_jaxpr/ppermute | solution.py:17
  348.4 15.1 %collective-permute-start.5 = (f32[128,512]{0,1:T(8,128)S(1)}, f32[128,512]{0,1:T(8,128)S(1)}, u32[]{:S(2)}, u32[]{:S(2)}) collective-permute-start(f32[128,512]{0,1:T(8,128)S(1)} %bitcast_add_fusion.6), channel_id=1, source_target_pairs={{0,8},{8,16},{16,24},{24,32},{32,40},{40,48},{48,56},{56,64},{64,7... | collective-permute-start | bytes 786440 | tf_op jit(solution)/shard_map/while/body/eval_jaxpr/ppermute | solution.py:17
  348.9 14.6 %collective-permute-start.6 = (f32[128,512]{0,1:T(8,128)S(1)}, f32[128,512]{0,1:T(8,128)S(1)}, u32[]{:S(2)}, u32[]{:S(2)}) collective-permute-start(f32[128,512]{0,1:T(8,128)S(1)} %bitcast_add_fusion.7), channel_id=1, source_target_pairs={{0,8},{8,16},{16,24},{24,32},{32,40},{40,48},{48,56},{56,64},{64,7... | collective-permute-start | bytes 786440 | tf_op jit(solution)/shard_map/while/body/eval_jaxpr/ppermute | solution.py:17
  349.1 14.4 %collective-permute-start.4 = (bf16[128,512]{1,0:T(8,128)(2,1)S(1)}, bf16[128,512]{1,0:T(8,128)(2,1)S(1)}, u32[]{:S(2)}, u32[]{:S(2)}) collective-permute-start(bf16[128,512]{1,0:T(8,128)(2,1)S(1)} %copy.259), channel_id=1, source_target_pairs={{0,8},{8,16},{16,24},{24,32},{32,40},{40,48},{48,56},{56,64},{64,7... | collective-permute-start | bytes 393224 | tf_op jit(solution)/shard_map/while/body/eval_jaxpr/ppermute | solution.py:17
  367.8 15.1 %collective-permute-start.5 = (f32[128,512]{0,1:T(8,128)S(1)}, f32[128,512]{0,1:T(8,128)S(1)}, u32[]{:S(2)}, u32[]{:S(2)}) collective-permute-start(f32[128,512]{0,1:T(8,128)S(1)} %bitcast_add_fusion.6), channel_id=1, source_target_pairs={{0,8},{8,16},{16,24},{24,32},{32,40},{40,48},{48,56},{56,64},{64,7... | collective-permute-start | bytes 786440 | tf_op jit(solution)/shard_map/while/body/eval_jaxpr/ppermute | solution.py:17
  368.3 14.6 %collective-permute-start.6 = (f32[128,512]{0,1:T(8,128)S(1)}, f32[128,512]{0,1:T(8,128)S(1)}, u32[]{:S(2)}, u32[]{:S(2)}) collective-permute-start(f32[128,512]{0,1:T(8,128)S(1)} %bitcast_add_fusion.7), channel_id=1, source_target_pairs={{0,8},{8,16},{16,24},{24,32},{32,40},{40,48},{48,56},{56,64},{64,7... | collective-permute-start | bytes 786440 | tf_op jit(solution)/shard_map/while/body/eval_jaxpr/ppermute | solution.py:17
  368.4 13.1 %collective-permute-start.3 = (bf16[128,512]{1,0:T(8,128)(2,1)S(1)}, bf16[128,512]{1,0:T(8,128)(2,1)S(1)}, u32[]{:S(2)}, u32[]{:S(2)}) collective-permute-start(bf16[128,512]{1,0:T(8,128)(2,1)S(1)} %copy.258), channel_id=1, source_target_pairs={{0,8},{8,16},{16,24},{24,32},{32,40},{40,48},{48,56},{56,64},{64,7... | collective-permute-start | bytes 393224 | tf_op jit(solution)/shard_map/while/body/eval_jaxpr/ppermute | solution.py:17
  368.5 14.4 %collective-permute-start.4 = (bf16[128,512]{1,0:T(8,128)(2,1)S(1)}, bf16[128,512]{1,0:T(8,128)(2,1)S(1)}, u32[]{:S(2)}, u32[]{:S(2)}) collective-permute-start(bf16[128,512]{1,0:T(8,128)(2,1)S(1)} %copy.259), channel_id=1, source_target_pairs={{0,8},{8,16},{16,24},{24,32},{32,40},{40,48},{48,56},{56,64},{64,7... | collective-permute-start | bytes 393224 | tf_op jit(solution)/shard_map/while/body/eval_jaxpr/ppermute | solution.py:17
  387.1 15.1 %collective-permute-start.5 = (f32[128,512]{0,1:T(8,128)S(1)}, f32[128,512]{0,1:T(8,128)S(1)}, u32[]{:S(2)}, u32[]{:S(2)}) collective-permute-start(f32[128,512]{0,1:T(8,128)S(1)} %bitcast_add_fusion.6), channel_id=1, source_target_pairs={{0,8},{8,16},{16,24},{24,32},{32,40},{40,48},{48,56},{56,64},{64,7... | collective-permute-start | bytes 786440 | tf_op jit(solution)/shard_map/while/body/eval_jaxpr/ppermute | solution.py:17
  387.7 14.6 %collective-permute-start.6 = (f32[128,512]{0,1:T(8,128)S(1)}, f32[128,512]{0,1:T(8,128)S(1)}, u32[]{:S(2)}, u32[]{:S(2)}) collective-permute-start(f32[128,512]{0,1:T(8,128)S(1)} %bitcast_add_fusion.7), channel_id=1, source_target_pairs={{0,8},{8,16},{16,24},{24,32},{32,40},{40,48},{48,56},{56,64},{64,7... | collective-permute-start | bytes 786440 | tf_op jit(solution)/shard_map/while/body/eval_jaxpr/ppermute | solution.py:17
  387.9 14.4 %collective-permute-start.4 = (bf16[128,512]{1,0:T(8,128)(2,1)S(1)}, bf16[128,512]{1,0:T(8,128)(2,1)S(1)}, u32[]{:S(2)}, u32[]{:S(2)}) collective-permute-start(bf16[128,512]{1,0:T(8,128)(2,1)S(1)} %copy.259), channel_id=1, source_target_pairs={{0,8},{8,16},{16,24},{24,32},{32,40},{40,48},{48,56},{56,64},{64,7... | collective-permute-start | bytes 393224 | tf_op jit(solution)/shard_map/while/body/eval_jaxpr/ppermute | solution.py:17
  406.5 15.1 %collective-permute-start.5 = (f32[128,512]{0,1:T(8,128)S(1)}, f32[128,512]{0,1:T(8,128)S(1)}, u32[]{:S(2)}, u32[]{:S(2)}) collective-permute-start(f32[128,512]{0,1:T(8,128)S(1)} %bitcast_add_fusion.6), channel_id=1, source_target_pairs={{0,8},{8,16},{16,24},{24,32},{32,40},{40,48},{48,56},{56,64},{64,7... | collective-permute-start | bytes 786440 | tf_op jit(solution)/shard_map/while/body/eval_jaxpr/ppermute | solution.py:17
  407.1 14.6 %collective-permute-start.6 = (f32[128,512]{0,1:T(8,128)S(1)}, f32[128,512]{0,1:T(8,128)S(1)}, u32[]{:S(2)}, u32[]{:S(2)}) collective-permute-start(f32[128,512]{0,1:T(8,128)S(1)} %bitcast_add_fusion.7), channel_id=1, source_target_pairs={{0,8},{8,16},{16,24},{24,32},{32,40},{40,48},{48,56},{56,64},{64,7... | collective-permute-start | bytes 786440 | tf_op jit(solution)/shard_map/while/body/eval_jaxpr/ppermute | solution.py:17
  407.2 14.4 %collective-permute-start.4 = (bf16[128,512]{1,0:T(8,128)(2,1)S(1)}, bf16[128,512]{1,0:T(8,128)(2,1)S(1)}, u32[]{:S(2)}, u32[]{:S(2)}) collective-permute-start(bf16[128,512]{1,0:T(8,128)(2,1)S(1)} %copy.259), channel_id=1, source_target_pairs={{0,8},{8,16},{16,24},{24,32},{32,40},{40,48},{48,56},{56,64},{64,7... | collective-permute-start | bytes 393224 | tf_op jit(solution)/shard_map/while/body/eval_jaxpr/ppermute | solution.py:17
  425.9 15.1 %collective-permute-start.5 = (f32[128,512]{0,1:T(8,128)S(1)}, f32[128,512]{0,1:T(8,128)S(1)}, u32[]{:S(2)}, u32[]{:S(2)}) collective-permute-start(f32[128,512]{0,1:T(8,128)S(1)} %bitcast_add_fusion.6), channel_id=1, source_target_pairs={{0,8},{8,16},{16,24},{24,32},{32,40},{40,48},{48,56},{56,64},{64,7... | collective-permute-start | bytes 786440 | tf_op jit(solution)/shard_map/while/body/eval_jaxpr/ppermute | solution.py:17
  426.5 14.6 %collective-permute-start.6 = (f32[128,512]{0,1:T(8,128)S(1)}, f32[128,512]{0,1:T(8,128)S(1)}, u32[]{:S(2)}, u32[]{:S(2)}) collective-permute-start(f32[128,512]{0,1:T(8,128)S(1)} %bitcast_add_fusion.7), channel_id=1, source_target_pairs={{0,8},{8,16},{16,24},{24,32},{32,40},{40,48},{48,56},{56,64},{64,7... | collective-permute-start | bytes 786440 | tf_op jit(solution)/shard_map/while/body/eval_jaxpr/ppermute | solution.py:17
  426.6 14.4 %collective-permute-start.4 = (bf16[128,512]{1,0:T(8,128)(2,1)S(1)}, bf16[128,512]{1,0:T(8,128)(2,1)S(1)}, u32[]{:S(2)}, u32[]{:S(2)}) collective-permute-start(bf16[128,512]{1,0:T(8,128)(2,1)S(1)} %copy.259), channel_id=1, source_target_pairs={{0,8},{8,16},{16,24},{24,32},{32,40},{40,48},{48,56},{56,64},{64,7... | collective-permute-start | bytes 393224 | tf_op jit(solution)/shard_map/while/body/eval_jaxpr/ppermute | solution.py:17
  445.3 15.1 %collective-permute-start.5 = (f32[128,512]{0,1:T(8,128)S(1)}, f32[128,512]{0,1:T(8,128)S(1)}, u32[]{:S(2)}, u32[]{:S(2)}) collective-permute-start(f32[128,512]{0,1:T(8,128)S(1)} %bitcast_add_fusion.6), channel_id=1, source_target_pairs={{0,8},{8,16},{16,24},{24,32},{32,40},{40,48},{48,56},{56,64},{64,7... | collective-permute-start | bytes 786440 | tf_op jit(solution)/shard_map/while/body/eval_jaxpr/ppermute | solution.py:17
  445.9 14.6 %collective-permute-start.6 = (f32[128,512]{0,1:T(8,128)S(1)}, f32[128,512]{0,1:T(8,128)S(1)}, u32[]{:S(2)}, u32[]{:S(2)}) collective-permute-start(f32[128,512]{0,1:T(8,128)S(1)} %bitcast_add_fusion.7), channel_id=1, source_target_pairs={{0,8},{8,16},{16,24},{24,32},{32,40},{40,48},{48,56},{56,64},{64,7... | collective-permute-start | bytes 786440 | tf_op jit(solution)/shard_map/while/body/eval_jaxpr/ppermute | solution.py:17
  446.0 14.4 %collective-permute-start.4 = (bf16[128,512]{1,0:T(8,128)(2,1)S(1)}, bf16[128,512]{1,0:T(8,128)(2,1)S(1)}, u32[]{:S(2)}, u32[]{:S(2)}) collective-permute-start(bf16[128,512]{1,0:T(8,128)(2,1)S(1)} %copy.259), channel_id=1, source_target_pairs={{0,8},{8,16},{16,24},{24,32},{32,40},{40,48},{48,56},{56,64},{64,7... | collective-permute-start | bytes 393224 | tf_op jit(solution)/shard_map/while/body/eval_jaxpr/ppermute | solution.py:17
  464.7 15.1 %collective-permute-start.5 = (f32[128,512]{0,1:T(8,128)S(1)}, f32[128,512]{0,1:T(8,128)S(1)}, u32[]{:S(2)}, u32[]{:S(2)}) collective-permute-start(f32[128,512]{0,1:T(8,128)S(1)} %bitcast_add_fusion.6), channel_id=1, source_target_pairs={{0,8},{8,16},{16,24},{24,32},{32,40},{40,48},{48,56},{56,64},{64,7... | collective-permute-start | bytes 786440 | tf_op jit(solution)/shard_map/while/body/eval_jaxpr/ppermute | solution.py:17
  465.2 14.6 %collective-permute-start.6 = (f32[128,512]{0,1:T(8,128)S(1)}, f32[128,512]{0,1:T(8,128)S(1)}, u32[]{:S(2)}, u32[]{:S(2)}) collective-permute-start(f32[128,512]{0,1:T(8,128)S(1)} %bitcast_add_fusion.7), channel_id=1, source_target_pairs={{0,8},{8,16},{16,24},{24,32},{32,40},{40,48},{48,56},{56,64},{64,7... | collective-permute-start | bytes 786440 | tf_op jit(solution)/shard_map/while/body/eval_jaxpr/ppermute | solution.py:17
  465.4 14.4 %collective-permute-start.4 = (bf16[128,512]{1,0:T(8,128)(2,1)S(1)}, bf16[128,512]{1,0:T(8,128)(2,1)S(1)}, u32[]{:S(2)}, u32[]{:S(2)}) collective-permute-start(bf16[128,512]{1,0:T(8,128)(2,1)S(1)} %copy.259), channel_id=1, source_target_pairs={{0,8},{8,16},{16,24},{24,32},{32,40},{40,48},{48,56},{56,64},{64,7... | collective-permute-start | bytes 393224 | tf_op jit(solution)/shard_map/while/body/eval_jaxpr/ppermute | solution.py:17
  484.1 15.1 %collective-permute-start.5 = (f32[128,512]{0,1:T(8,128)S(1)}, f32[128,512]{0,1:T(8,128)S(1)}, u32[]{:S(2)}, u32[]{:S(2)}) collective-permute-start(f32[128,512]{0,1:T(8,128)S(1)} %bitcast_add_fusion.6), channel_id=1, source_target_pairs={{0,8},{8,16},{16,24},{24,32},{32,40},{40,48},{48,56},{56,64},{64,7... | collective-permute-start | bytes 786440 | tf_op jit(solution)/shard_map/while/body/eval_jaxpr/ppermute | solution.py:17
  484.6 14.6 %collective-permute-start.6 = (f32[128,512]{0,1:T(8,128)S(1)}, f32[128,512]{0,1:T(8,128)S(1)}, u32[]{:S(2)}, u32[]{:S(2)}) collective-permute-start(f32[128,512]{0,1:T(8,128)S(1)} %bitcast_add_fusion.7), channel_id=1, source_target_pairs={{0,8},{8,16},{16,24},{24,32},{32,40},{40,48},{48,56},{56,64},{64,7... | collective-permute-start | bytes 786440 | tf_op jit(solution)/shard_map/while/body/eval_jaxpr/ppermute | solution.py:17
  484.8 14.4 %collective-permute-start.4 = (bf16[128,512]{1,0:T(8,128)(2,1)S(1)}, bf16[128,512]{1,0:T(8,128)(2,1)S(1)}, u32[]{:S(2)}, u32[]{:S(2)}) collective-permute-start(bf16[128,512]{1,0:T(8,128)(2,1)S(1)} %copy.259), channel_id=1, source_target_pairs={{0,8},{8,16},{16,24},{24,32},{32,40},{40,48},{48,56},{56,64},{64,7... | collective-permute-start | bytes 393224 | tf_op jit(solution)/shard_map/while/body/eval_jaxpr/ppermute | solution.py:17
  503.5 15.1 %collective-permute-start.5 = (f32[128,512]{0,1:T(8,128)S(1)}, f32[128,512]{0,1:T(8,128)S(1)}, u32[]{:S(2)}, u32[]{:S(2)}) collective-permute-start(f32[128,512]{0,1:T(8,128)S(1)} %bitcast_add_fusion.6), channel_id=1, source_target_pairs={{0,8},{8,16},{16,24},{24,32},{32,40},{40,48},{48,56},{56,64},{64,7... | collective-permute-start | bytes 786440 | tf_op jit(solution)/shard_map/while/body/eval_jaxpr/ppermute | solution.py:17
  504.0 14.6 %collective-permute-start.6 = (f32[128,512]{0,1:T(8,128)S(1)}, f32[128,512]{0,1:T(8,128)S(1)}, u32[]{:S(2)}, u32[]{:S(2)}) collective-permute-start(f32[128,512]{0,1:T(8,128)S(1)} %bitcast_add_fusion.7), channel_id=1, source_target_pairs={{0,8},{8,16},{16,24},{24,32},{32,40},{40,48},{48,56},{56,64},{64,7... | collective-permute-start | bytes 786440 | tf_op jit(solution)/shard_map/while/body/eval_jaxpr/ppermute | solution.py:17
  504.2 14.4 %collective-permute-start.4 = (bf16[128,512]{1,0:T(8,128)(2,1)S(1)}, bf16[128,512]{1,0:T(8,128)(2,1)S(1)}, u32[]{:S(2)}, u32[]{:S(2)}) collective-permute-start(bf16[128,512]{1,0:T(8,128)(2,1)S(1)} %copy.259), channel_id=1, source_target_pairs={{0,8},{8,16},{16,24},{24,32},{32,40},{40,48},{48,56},{56,64},{64,7... | collective-permute-start | bytes 393224 | tf_op jit(solution)/shard_map/while/body/eval_jaxpr/ppermute | solution.py:17
  522.8 15.1 %collective-permute-start.5 = (f32[128,512]{0,1:T(8,128)S(1)}, f32[128,512]{0,1:T(8,128)S(1)}, u32[]{:S(2)}, u32[]{:S(2)}) collective-permute-start(f32[128,512]{0,1:T(8,128)S(1)} %bitcast_add_fusion.6), channel_id=1, source_target_pairs={{0,8},{8,16},{16,24},{24,32},{32,40},{40,48},{48,56},{56,64},{64,7... | collective-permute-start | bytes 786440 | tf_op jit(solution)/shard_map/while/body/eval_jaxpr/ppermute | solution.py:17
  523.4 14.6 %collective-permute-start.6 = (f32[128,512]{0,1:T(8,128)S(1)}, f32[128,512]{0,1:T(8,128)S(1)}, u32[]{:S(2)}, u32[]{:S(2)}) collective-permute-start(f32[128,512]{0,1:T(8,128)S(1)} %bitcast_add_fusion.7), channel_id=1, source_target_pairs={{0,8},{8,16},{16,24},{24,32},{32,40},{40,48},{48,56},{56,64},{64,7... | collective-permute-start | bytes 786440 | tf_op jit(solution)/shard_map/while/body/eval_jaxpr/ppermute | solution.py:17
  523.6 14.4 %collective-permute-start.4 = (bf16[128,512]{1,0:T(8,128)(2,1)S(1)}, bf16[128,512]{1,0:T(8,128)(2,1)S(1)}, u32[]{:S(2)}, u32[]{:S(2)}) collective-permute-start(bf16[128,512]{1,0:T(8,128)(2,1)S(1)} %copy.259), channel_id=1, source_target_pairs={{0,8},{8,16},{16,24},{24,32},{32,40},{40,48},{48,56},{56,64},{64,7... | collective-permute-start | bytes 393224 | tf_op jit(solution)/shard_map/while/body/eval_jaxpr/ppermute | solution.py:17
  542.2 15.1 %collective-permute-start.5 = (f32[128,512]{0,1:T(8,128)S(1)}, f32[128,512]{0,1:T(8,128)S(1)}, u32[]{:S(2)}, u32[]{:S(2)}) collective-permute-start(f32[128,512]{0,1:T(8,128)S(1)} %bitcast_add_fusion.6), channel_id=1, source_target_pairs={{0,8},{8,16},{16,24},{24,32},{32,40},{40,48},{48,56},{56,64},{64,7... | collective-permute-start | bytes 786440 | tf_op jit(solution)/shard_map/while/body/eval_jaxpr/ppermute | solution.py:17
  542.8 14.6 %collective-permute-start.6 = (f32[128,512]{0,1:T(8,128)S(1)}, f32[128,512]{0,1:T(8,128)S(1)}, u32[]{:S(2)}, u32[]{:S(2)}) collective-permute-start(f32[128,512]{0,1:T(8,128)S(1)} %bitcast_add_fusion.7), channel_id=1, source_target_pairs={{0,8},{8,16},{16,24},{24,32},{32,40},{40,48},{48,56},{56,64},{64,7... | collective-permute-start | bytes 786440 | tf_op jit(solution)/shard_map/while/body/eval_jaxpr/ppermute | solution.py:17
  542.9 14.4 %collective-permute-start.4 = (bf16[128,512]{1,0:T(8,128)(2,1)S(1)}, bf16[128,512]{1,0:T(8,128)(2,1)S(1)}, u32[]{:S(2)}, u32[]{:S(2)}) collective-permute-start(bf16[128,512]{1,0:T(8,128)(2,1)S(1)} %copy.259), channel_id=1, source_target_pairs={{0,8},{8,16},{16,24},{24,32},{32,40},{40,48},{48,56},{56,64},{64,7... | collective-permute-start | bytes 393224 | tf_op jit(solution)/shard_map/while/body/eval_jaxpr/ppermute | solution.py:17
  561.6 15.1 %collective-permute-start.5 = (f32[128,512]{0,1:T(8,128)S(1)}, f32[128,512]{0,1:T(8,128)S(1)}, u32[]{:S(2)}, u32[]{:S(2)}) collective-permute-start(f32[128,512]{0,1:T(8,128)S(1)} %bitcast_add_fusion.6), channel_id=1, source_target_pairs={{0,8},{8,16},{16,24},{24,32},{32,40},{40,48},{48,56},{56,64},{64,7... | collective-permute-start | bytes 786440 | tf_op jit(solution)/shard_map/while/body/eval_jaxpr/ppermute | solution.py:17
  562.2 14.6 %collective-permute-start.6 = (f32[128,512]{0,1:T(8,128)S(1)}, f32[128,512]{0,1:T(8,128)S(1)}, u32[]{:S(2)}, u32[]{:S(2)}) collective-permute-start(f32[128,512]{0,1:T(8,128)S(1)} %bitcast_add_fusion.7), channel_id=1, source_target_pairs={{0,8},{8,16},{16,24},{24,32},{32,40},{40,48},{48,56},{56,64},{64,7... | collective-permute-start | bytes 786440 | tf_op jit(solution)/shard_map/while/body/eval_jaxpr/ppermute | solution.py:17
  562.3 14.4 %collective-permute-start.4 = (bf16[128,512]{1,0:T(8,128)(2,1)S(1)}, bf16[128,512]{1,0:T(8,128)(2,1)S(1)}, u32[]{:S(2)}, u32[]{:S(2)}) collective-permute-start(bf16[128,512]{1,0:T(8,128)(2,1)S(1)} %copy.259), channel_id=1, source_target_pairs={{0,8},{8,16},{16,24},{24,32},{32,40},{40,48},{48,56},{56,64},{64,7... | collective-permute-start | bytes 393224 | tf_op jit(solution)/shard_map/while/body/eval_jaxpr/ppermute | solution.py:17
  (66 other events, 754.6 us)
Sparse Core Ops, SparseCore 0:
  9.0 41.5 all-gather.1
  591.5 41.5 reduce-scatter.1
where the time goes:
time: 644 us; the launch traced here: 642 us
  waiting for transfers between devices  386 us (60%)
  other arithmetic  122 us (19%)
  local copies, waits for them, and re-layouts  64.3 us (10%)
  matrix products  42.5 us (7%)
  between operations  13.8 us (2%)
  starting transfers between devices  8.22 us (1%)
    ppermute x107, waiting for transfers between devices, shifted(): return lax.ppermute(value, axis, pairs)  344 us
    add x92, other arithmetic, block_positions(): jnp.where(row_index < within, stretch_pair[0], stretch_pair[1]) * within  115 us
    reduce_scatter x1, waiting for transfers between devices, body(): return lax.psum_scatter(running, 'heads', scatter_dimension=0, tiled=True)  41.7 us
    slice x46, local copies, waits for them, and re-layouts, block_positions(): stretch_pair[0]  27.9 us
    dynamic_slice x46, local copies, waits for them, and re-layouts, block_positions(): lax.dynamic_slice_in_dim(stretch_order, 2 * block_index, 2, 0)  23.9 us
  transfers between devices with their start and end apart: 109, of which 77 were waited for; matrix products, arithmetic and copies ran while one was open for 24% of the time, Pallas kernels for 0%

commit v1 on v0

v1 whole, which is shorter than its diff:
```python
import functools

import jax
import jax.numpy as jnp
from jax import lax
from jax.experimental import pallas as pl
from jax.experimental.pallas import tpu as pltpu
from jax.sharding import PartitionSpec as P

MESH = pl.DeviceIdType.MESH
HDIM = 128
WIDTH = 256
LAMBDA_INIT = 0.8
EPSILON = 1e-05
MASKED = -1e30
SCALE = HDIM**-0.5
LOG2E = 1.4426950408889634
F32 = jnp.float32
BF16 = jnp.bfloat16


def mm(a, b, dims=((1,), (0,))):
    return lax.dot_general(a, b, (dims, ((), ())), preferred_element_type=F32)


NT = ((1,), (1,))
TN = ((0,), (0,))


def kernel(
    order, lam, gain, qh, kh, vh, og, wq, wk, wv, wo, out,
    kb, vb, qb, gs, gb, ogb, wob, wb, ls, lr, st, qt, d0, ot, gacc, gt, gn, dq,
    sibs, sibr, own, ys, yr, yf, dqs, dks, rb, pa, xs_, xr, xf, zs, zr,
    wsem, lsem, ssem, rsem,
):
    ctx = lax.axis_index("ctx")
    hd = lax.axis_index("heads")
    hi = lax.div(ctx, 8)
    y = lax.rem(lax.div(ctx, 2), 4)
    c = lax.rem(ctx, 2)
    lo = lax.div(hd, 4)
    x = lax.rem(hd, 4)

    def dev(hi_, y_, c_, lo_, x_):
        return (hi_ * 8 + y_ * 2 + c_, lo_ * 4 + x_)

    sib = dev(hi, y, 1 - c, lo, x)
    yp = dev(hi, lax.rem(y + 1, 4), c, lo, x)
    ym = dev(hi, lax.rem(y + 3, 4), c, lo, x)
    xp = dev(hi, y, c, lo, lax.rem(x + 1, 4))
    xm = dev(hi, y, c, lo, lax.rem(x + 3, 4))
    zn = [dev(a, y, c, 1 - lo, x) for a in range(2)]
    partner = dev(hi, y, c, 1 - lo, x)

    local = []
    own_og = pltpu.make_async_copy(og, ogb.at[0, 0], lsem.at[0])
    own_og.start()
    wo_copies = {}
    for s in range(4):
        for r in range(2):
            block = lax.rem(lo + r, 2) * 4 + lax.rem(x + s, 4)
            at = pl.ds(pl.multiple_of(block * 512, 512), 512)
            cp = pltpu.make_async_copy(wo.at[:, at], wob.at[r, s], wsem.at[3, r, s])
            cp.start()
            wo_copies[r, s] = cp
    w_copies = {}
    for k, w in enumerate((wq, wk, wv)):
        for s in (2, 1, 3, 0):
            for r in (1, 0):
                block = lax.rem(lo + r, 2) * 4 + lax.rem(x + s, 4)
                at = pl.ds(pl.multiple_of(block * 512, 512), 512)
                cp = pltpu.make_async_copy(w.at[at, :], wb.at[k, r, s], wsem.at[k, r, s])
                cp.start()
                w_copies[k, r, s] = cp

    ls[...] = jnp.full((8, 128), lam[hi], F32)

    barrier = pltpu.get_barrier_semaphore()
    for d in (sib, yp, ym, xp, xm, zn[0], zn[1]):
        pl.semaphore_signal(barrier, inc=1, device_id=d, device_id_type=MESH)
    pl.semaphore_wait(barrier, 7)

    used = [0]
    sent = []

    def send(src, dst, recv, to):
        n = used[0]
        used[0] += 1
        cp = pltpu.make_async_remote_copy(
            src_ref=src, dst_ref=dst, send_sem=ssem.at[n], recv_sem=rsem.at[recv],
            device_id=to, device_id_type=MESH,
        )
        cp.start()
        sent.append(cp)

    def arrived(dst, recv):
        pltpu.make_async_remote_copy(
            src_ref=dst, dst_ref=dst, send_sem=ssem.at[0], recv_sem=rsem.at[recv],
            device_id=sib, device_id_type=MESH,
        ).wait_recv()

    names = {}

    def num(*key):
        if key not in names:
            names[key] = len(names)
        return names[key]

    for kind in ("k", "v", "q", "g", "dq", "dk", "dv"):
        for a in range(2):
            num("z", kind, a)

    def zsend(src, dst, kind, a):
        send(src, dst, num("z", kind, 0) + hi, zn[a])

    mine = pl.ds(pl.multiple_of(hi * 128, 128), 128)
    for a in range(2):
        zsend(kh.at[:, a * 256 : a * 256 + 256], kb.at[0, 0, mine], "k", a)
    send(og, ogb.at[0, 3], num("og", 0, 3), xp)
    send(og, ogb.at[0, 1], num("og", 0, 1), xm)
    for a in range(2):
        zsend(vh.at[:, a * 256 : a * 256 + 256], vb.at[0, 0, mine], "v", a)
    send(og, ogb.at[1, 0], num("og", 1, 0), partner)
    for a in range(2):
        zsend(qh.at[:, a * 256 : a * 256 + 256], qb.at[mine], "q", a)
    send(ls, lr, num("lam"), partner)

    def first(buf, kind):
        for a in range(2):
            arrived(buf.at[0, 0, pl.ds(a * 128, 128)], num("z", kind, a))
        send(buf.at[0, 0], buf.at[3, 0], num(kind, 3, 0), yp)
        send(buf.at[0, 0], buf.at[1, 0], num(kind, 1, 0), ym)
        send(buf.at[0, 0], buf.at[0, 1], num(kind, 0, 1), sib)

    def relay(buf, kind):
        lower, upper = pl.ds(0, 128), pl.ds(128, 128)
        arrived(buf.at[3, 0], num(kind, 3, 0))
        send(buf.at[3, 0, lower], buf.at[2, 0, lower], num(kind, 2, 0, 0), yp)
        arrived(buf.at[1, 0], num(kind, 1, 0))
        send(buf.at[1, 0, upper], buf.at[2, 0, upper], num(kind, 2, 0, 1), ym)
        send(buf.at[3, 0], buf.at[3, 1], num(kind, 3, 1), sib)
        send(buf.at[1, 0], buf.at[1, 1], num(kind, 1, 1), sib)

    def last(buf, kind):
        arrived(buf.at[2, 0, pl.ds(0, 128)], num(kind, 2, 0, 0))
        arrived(buf.at[2, 0, pl.ds(128, 128)], num(kind, 2, 0, 1))
        send(buf.at[2, 0], buf.at[2, 1], num(kind, 2, 1), sib)

    first(kb, "k")
    first(vb, "v")

    lane = lax.broadcasted_iota(jnp.int32, (64, 256), 1)
    row = lax.broadcasted_iota(jnp.int32, (64, 256), 0)

    def stretch(hi_, s, r, half):
        block = hi_ * 8 + lax.rem(y + s, 4) * 2 + lax.rem(c + r, 2)
        return order[block * 2 + half]

    qs = [stretch(h, 0, 0, half) for h in range(2) for half in range(2)]
    qstretch = jnp.where(
        lane < 128,
        jnp.where(lane < 64, qs[0], qs[1]),
        jnp.where(lane < 192, qs[2], qs[3]),
    )
    d0[...] = row - qstretch * 64 - lax.rem(lane, 64)

    own_og.wait()
    arrived(ogb.at[1, 0], num("og", 1, 0))
    send(ogb.at[1, 0], ogb.at[1, 3], num("og", 1, 3), xp)
    send(ogb.at[1, 0], ogb.at[1, 1], num("og", 1, 1), xm)

    for a in range(2):
        arrived(qb.at[pl.ds(a * 128, 128)], num("z", "q", a))
    for j in range(2):
        qt[j] = jnp.transpose(qb[:, j * 128 : j * 128 + 128].astype(F32)).astype(BF16)

    def scores(s, r, peak):
        i = s * 2 + r
        peaks = list(peak)
        for j in range(2):
            sc = mm(kb[s, r, :, j * 128 : j * 128 + 128], qt[j]) * (SCALE * LOG2E)
            for n in range(4):
                threshold = stretch(n // 2, s, r, n % 2) * -64
                part = jnp.where(d0[...] <= threshold, sc[n * 64 : n * 64 + 64], MASKED)
                st[j, i, n * 64 : n * 64 + 64] = part
                peaks[j] = jnp.maximum(peaks[j], jnp.max(part.reshape(8, 8, 256), axis=0))
        return tuple(peaks)

    def gdot(r, s, start=False):
        wo_copies[r, s].wait()
        term = mm(wob[r, s], ogb[r, s], NT)
        gacc[...] = term if start else gacc[...] + term

    peak = (jnp.full((8, 256), MASKED, F32),) * 2
    peak = scores(0, 0, peak)
    gdot(0, 0, True)
    relay(kb, "k")
    arrived(kb.at[0, 1], num("k", 0, 1))
    peak = scores(0, 1, peak)
    gdot(1, 0)
    arrived(ogb.at[0, 3], num("og", 0, 3))
    send(ogb.at[0, 3], ogb.at[0, 2], num("og", 0, 2), xp)
    relay(vb, "v")
    arrived(ogb.at[0, 1], num("og", 0, 1))
    gdot(0, 3)
    gdot(0, 1)
    peak = scores(1, 0, peak)
    peak = scores(3, 0, peak)
    arrived(kb.at[1, 1], num("k", 1, 1))
    peak = scores(1, 1, peak)
    arrived(kb.at[3, 1], num("k", 3, 1))
    peak = scores(3, 1, peak)
    arrived(ogb.at[1, 1], num("og", 1, 1))
    send(ogb.at[1, 1], ogb.at[1, 2], num("og", 1, 2), xm)
    last(kb, "k")
    arrived(ogb.at[1, 3], num("og", 1, 3))
    gdot(1, 3)
    gdot(1, 1)
    peak = scores(2, 0, peak)
    arrived(kb.at[2, 1], num("k", 2, 1))
    peak = scores(2, 1, peak)
    last(vb, "v")
    arrived(ogb.at[0, 2], num("og", 0, 2))
    gdot(0, 2)
    arrived(ogb.at[1, 2], num("og", 1, 2))
    gdot(1, 2)
    for a in range(2):
        gs[a] = gacc[a * 256 : a * 256 + 256].astype(BF16)
        zsend(gs.at[a], gb.at[hi], "g", a)

    for s in (0, 1, 3, 2):
        arrived(vb.at[s, 1], num("v", s, 1))

    tops = [jnp.max(p, axis=0, keepdims=True) for p in peak]
    ot[...] = jnp.zeros_like(ot)

    def weigh(i, sums):
        s, r = lax.div(i, 2), lax.rem(i, 2)
        sums = list(sums)
        parts = []
        for j in range(2):
            p = jnp.exp2(st[j, i] - tops[j])
            st[j, i] = p
            sums[j] = sums[j] + jnp.sum(p.reshape(32, 8, 256), axis=0)
            parts.append(p.astype(BF16))
        ot[...] += mm(vb[s, r], jnp.concatenate(parts, axis=1), TN)
        return tuple(sums)

    sums = lax.fori_loop(0, 8, weigh, (jnp.zeros((8, 256), F32),) * 2)
    inv = [1.0 / jnp.sum(t, axis=0, keepdims=True) for t in sums]

    arrived(lr, num("lam"))
    lam_row = jnp.concatenate([lr[0:1, :], lr[0:1, :]], axis=1)
    gain_t = jnp.transpose(jnp.broadcast_to(gain[...], (128, 256)))
    gain_t = jnp.concatenate([gain_t, gain_t], axis=1)
    for a in range(2):
        arrived(gb.at[a], num("z", "g", a))

    o1 = ot[:, :256] * inv[0]
    o2 = ot[:, 256:] * inv[1]
    combined = o1 - lam_row * o2
    rms = jnp.sqrt(jnp.mean(combined * combined, axis=0, keepdims=True) + EPSILON)
    inv_rms = 1.0 / rms
    normed = combined * inv_rms
    g = jnp.concatenate([gb[0], gb[1]], axis=1).astype(F32) * (gain_t * (1.0 - LAMBDA_INIT))
    grad = ((g - normed * jnp.mean(g * normed, axis=0, keepdims=True)) * inv_rms).astype(BF16)
    gt[...] = grad
    grad32 = grad.astype(F32)
    gn[...] = jnp.transpose(grad32).astype(BF16)
    stat1 = jnp.sum(grad32 * (ot[:, :256] * inv[0]), axis=0, keepdims=True)
    stat2 = jnp.sum(grad32 * (ot[:, 256:] * inv[1]), axis=0, keepdims=True)
    inv1 = inv[0]
    inv2 = inv[1] * lam_row

    dq[...] = jnp.zeros_like(dq)

    def backward(s, r):
        i = s * 2 + r
        dp = mm(vb[s, r], gt[...])
        p1 = st[0, i] * inv1
        p2 = st[1, i] * inv2
        mixed = (p1 - p2).astype(BF16)
        ds1 = (p1 * (dp - stat1)).astype(BF16)
        ds2 = (p2 * (dp - stat2)).astype(BF16)
        dv = mm(mixed, gn[...])
        dk1 = mm(ds1, qb[:, 0:128]) * SCALE
        dk2 = mm(ds2, qb[:, 128:256]) * -SCALE
        dq[0] += mm(kb[s, r, :, 0:128], ds1, TN)
        dq[1] += mm(kb[s, r, :, 128:256], ds2, TN)
        for part, at in ((dk1, 0), (dk2, 128), (dv, 256)):
            cols = pl.ds(at, part.shape[1])
            if r:
                sibs[s, :, cols] = part.astype(BF16)
            else:
                own[s, :, cols] = part
        if r:
            send(sibs.at[s], sibr.at[s], num("sib", s), sib)

    lower, upper = pl.ds(0, 128), pl.ds(128, 128)

    def total(s, part):
        return own[s, part] + sibr[s, part].astype(F32)

    backward(2, 1)
    backward(2, 0)
    backward(1, 1)
    backward(3, 1)
    arrived(sibr.at[2], num("sib", 2))
    ys[0] = total(2, pl.ds(0, 256)).astype(BF16)
    send(ys.at[0, lower], yr.at[0], num("yr", 0), yp)
    send(ys.at[0, upper], yr.at[1], num("yr", 1), ym)
    backward(1, 0)
    arrived(sibr.at[1], num("sib", 1))
    ys[1, upper] = total(1, upper).astype(BF16)
    send(ys.at[1, upper], yf.at[0, upper], num("yf", 0, 1), yp)
    backward(3, 0)
    arrived(sibr.at[3], num("sib", 3))
    ys[2, lower] = total(3, lower).astype(BF16)
    send(ys.at[2, lower], yf.at[1, lower], num("yf", 1, 0), ym)
    backward(0, 1)
    arrived(yr.at[0], num("yr", 0))
    ys[1, lower] = (total(1, lower) + yr[0].astype(F32)).astype(BF16)
    send(ys.at[1, lower], yf.at[0, lower], num("yf", 0, 0), yp)
    arrived(yr.at[1], num("yr", 1))
    ys[2, upper] = (total(3, upper) + yr[1].astype(F32)).astype(BF16)
    send(ys.at[2, upper], yf.at[1, upper], num("yf", 1, 1), ym)
    backward(0, 0)
    for a in range(2):
        for j, sign in ((0, SCALE), (1, -SCALE)):
            dqs[a, j * 128 : j * 128 + 128] = (dq[j, :, a * 128 : a * 128 + 128] * sign).astype(BF16)
    heads_rows = pl.ds(pl.multiple_of(hi * 256, 256), 256)
    for a in range(2):
        zsend(dqs.at[a], rb.at[0, heads_rows], "dq", a)
    arrived(sibr.at[0], num("sib", 0))
    for a in range(2):
        part = pl.ds(a * 128, 128)
        for d in range(2):
            arrived(yf.at[d, part], num("yf", d, a))
        whole = total(0, part) + yf[0, part].astype(F32) + yf[1, part].astype(F32)
        dks[a] = jnp.transpose(whole).astype(BF16)
        zsend(dks.at[a, pl.ds(0, 256)], rb.at[1, heads_rows], "dk", a)
        zsend(dks.at[a, pl.ds(256, 256)], rb.at[2, heads_rows], "dv", a)

    for a in range(2):
        arrived(rb.at[0, pl.ds(a * 256, 256)], num("z", "dq", a))
    blocks = [(1, 2), (0, 2), (1, 1), (0, 3), (0, 1), (1, 3), (1, 0), (0, 0)]
    for r, s in blocks:
        w_copies[0, r, s].wait()
        pa[r, s] = mm(wb[0, r, s], rb[0])
    for a in range(2):
        arrived(rb.at[1, pl.ds(a * 256, 256)], num("z", "dk", a))
        arrived(rb.at[2, pl.ds(a * 256, 256)], num("z", "dv", a))

    def project(r, s):
        w_copies[1, r, s].wait()
        w_copies[2, r, s].wait()
        return pa[r, s] + mm(wb[1, r, s], rb[1]) + mm(wb[2, r, s], rb[2])

    xs_[1, 1] = project(1, 2).astype(BF16)
    send(xs_.at[1, 1], xr.at[1], num("xr", 1), xp)
    xs_[0, 1] = project(0, 2).astype(BF16)
    send(xs_.at[0, 1], xr.at[0], num("xr", 0), xm)
    xs_[1, 2] = project(1, 3).astype(BF16)
    send(xs_.at[1, 2], xf.at[1, 1], num("xf", 1, 1), xm)
    pa[1, 1] = project(1, 1)
    arrived(xr.at[1], num("xr", 1))
    xs_[1, 0] = (pa[1, 1] + xr[1].astype(F32)).astype(BF16)
    send(xs_.at[1, 0], xf.at[0, 1], num("xf", 0, 1), xp)
    xs_[0, 0] = project(0, 1).astype(BF16)
    send(xs_.at[0, 0], xf.at[0, 0], num("xf", 0, 0), xp)
    pa[0, 3] = project(0, 3)
    arrived(xr.at[0], num("xr", 0))
    xs_[0, 2] = (pa[0, 3] + xr[0].astype(F32)).astype(BF16)
    send(xs_.at[0, 2], xf.at[1, 0], num("xf", 1, 0), xm)
    pa[1, 0] = project(1, 0)
    pa[0, 0] = project(0, 0)
    arrived(xf.at[1, 1], num("xf", 1, 1))
    arrived(xf.at[0, 1], num("xf", 0, 1))
    zs[...] = (pa[1, 0] + xf[0, 1].astype(F32) + xf[1, 1].astype(F32)).astype(BF16)
    send(zs, zr, num("zr"), partner)
    arrived(xf.at[0, 0], num("xf", 0, 0))
    arrived(xf.at[1, 0], num("xf", 1, 0))
    arrived(zr, num("zr"))
    out[...] = (pa[0, 0] + xf[0, 0].astype(F32)) + (xf[1, 0].astype(F32) + zr[...].astype(F32))

    for cp in sent:
        cp.wait_send()


def body(order, qh, kh, vh, og, wq, wk, wv, wo, lam, gain):
    any_ = pl.BlockSpec(memory_space=pl.ANY)
    smem = pl.BlockSpec(memory_space=pltpu.SMEM)
    vmem = pl.BlockSpec(memory_space=pltpu.VMEM)
    v = pltpu.VMEM
    return pl.pallas_call(
        kernel,
        out_shape=jax.ShapeDtypeStruct((512, 128), F32),
        in_specs=[smem, smem, vmem] + [any_] * 8,
        out_specs=vmem,
        scratch_shapes=[
            v((4, 2, 256, 256), BF16),
            v((4, 2, 256, 256), BF16),
            v((256, 256), BF16),
            v((2, 256, 128), BF16),
            v((2, 256, 128), BF16),
            v((2, 4, 128, 512), BF16),
            v((2, 4, 512, 512), BF16),
            v((3, 2, 4, 512, 512), BF16),
            v((8, 128), F32),
            v((8, 128), F32),
            v((2, 8, 256, 256), F32),
            v((2, 128, 256), BF16),
            v((64, 256), jnp.int32),
            v((256, 512), F32),
            v((512, 128), F32),
            v((256, 256), BF16),
            v((256, 256), BF16),
            v((2, 128, 256), F32),
            v((4, 256, 512), BF16),
            v((4, 256, 512), BF16),
            v((4, 256, 512), F32),
            v((3, 256, 512), BF16),
            v((2, 128, 512), BF16),
            v((2, 256, 512), BF16),
            v((2, 256, 128), BF16),
            v((2, 512, 128), BF16),
            v((3, 512, 128), BF16),
            v((2, 4, 512, 128), F32),
            v((2, 3, 512, 128), BF16),
            v((2, 512, 128), BF16),
            v((2, 2, 512, 128), BF16),
            v((512, 128), BF16),
            v((512, 128), BF16),
            pltpu.SemaphoreType.DMA((4, 2, 4)),
            pltpu.SemaphoreType.DMA((1,)),
            pltpu.SemaphoreType.DMA((72,)),
            pltpu.SemaphoreType.DMA((72,)),
        ],
        compiler_params=pltpu.CompilerParams(
            collective_id=0, has_side_effects=True, vmem_limit_bytes=56 * 2**20
        ),
        name="differential_attention_backward",
    )(order, lam, gain.reshape(1, 256), qh, kh, vh, og, wq, wk, wv, wo)


def solution(mesh):
    in_specs = (
        P(),
        P("ctx", "heads"),
        P("ctx", "heads"),
        P("ctx", "heads"),
        P("ctx", "heads"),
        P(None, "heads"),
        P(None, "heads"),
        P(None, "heads"),
        P("heads", None),
        P("heads"),
        P(),
    )
    out_specs = P("heads", "ctx")
    return jax.shard_map(body, mesh=mesh, in_specs=in_specs, out_specs=out_specs, check_vma=False)
```

time: 644 us -> 65.4 us (0.10)
  waiting for transfers between devices: 386 us -> 0 us
  other arithmetic: 122 us -> 0 us
  Pallas kernels: 0 us -> 63 us
  local copies, waits for them, and re-layouts: 64.3 us -> 1.67 us
  matrix products: 42.5 us -> 0 us
  between operations: 13.8 us -> 0.01 us
  starting transfers between devices: 8.22 us -> 0 us
    ppermute x107 -> x0, waiting for transfers between devices: 344 us -> none  [shifted(): return lax.ppermute(value, axis, pairs)]
    add x140 -> x0, other arithmetic: 116 us -> none  [the longest x92 115 us: block_positions(): jnp.where(row_index < within, stretch_pair[0], stretch_pair[1]) * within]
    pallas_call x0 -> x1, Pallas kernels: none -> 63 us  [body(): pl.pallas_call(kernel, out_shape=jax.ShapeDtypeStruct((512, 128), F32), i...]
    reduce_scatter x1 -> x0, waiting for transfers between devices: 41.7 us -> none  [body(): return lax.psum_scatter(running, 'heads', scatter_dimension=0, tiled=True)]
    dot_general x116 -> x0, matrix products: 38.7 us -> none  [the longest x3 8.15 us: body(): lax.dot_general(projection, gradient, (((1,), (1,)), ((), ())), preferred...]
    slice x46 -> x0, local copies, waits for them, and re-layouts: 27.9 us -> none  [block_positions(): stretch_pair[0]]
    dynamic_slice x46 -> x0, local copies, waits for them, and re-layouts: 23.9 us -> none  [block_positions(): lax.dynamic_slice_in_dim(stretch_order, 2 * block_index, 2, 0)]
    ppermute x107 -> x0, starting transfers between devices: 8.18 us -> none  [shifted(): return lax.ppermute(value, axis, pairs)]
  transfers between devices with their start and end apart: 109 -> 0, of which waited for: 77 -> 0; matrix products, arithmetic and copies ran while one was open for 24% -> 0% of each run, Pallas kernels for 0% -> 0%
where the time goes in v1:
time: 65.4 us; the launch traced here: 64.7 us
  Pallas kernels  63 us (96%)
  local copies, waits for them, and re-layouts  1.67 us (3%)
    pallas_call x1, Pallas kernels, body(): pl.pallas_call(kernel, out_shape=jax.ShapeDtypeStruct((512, 128), F32), i...  63 us
    unnamed x1, local copies, waits for them, and re-layouts  1.67 us

profile of v1, /device:TPU:0, one launch (start us, length us, event | category | flops | bytes accessed | tf_op | source)
XLA Modules:
  0.0 64.7 jit_solution(9137049342003552616)
XLA Ops:
  0.0 63.0 %differential_attention_backward.1 = f32[512,128]{1,0:T(8,128)} custom-call(s32[32]{0:T(128)} %order.1, f32[2]{0:T(128)} %lam.1, f32[1,256]{1,0:T(1,128)} %bitcast.1, bf16[128,512]{1,0:T(8,128)(2,1)} %qh.1, bf16[128,512]{1,0:T(8,128)(2,1)} %kh.1, bf16[128,512]{1,0:T(8,128)(2,1)} %vh.1, bf16[128,512]{1,0:T(8,128)(2,1)} %og.1, bf16[4096,512]{1,0:T(8,128)(2,1)} %wq.1, ...), custom_call_target="tpu_custom_call" | custom-call | tf_op jit(solution)/shard_map/differential_attention_backward/pallas_call | solution.py:395
  63.0 1.7 %copy.13 = f32[512,128]{1,0:T(8,128)} copy(f32[512,128]{1,0:T(8,128)} %differential_attention_backward.1) | data formatting | bytes 524288

commit v2 on v1

v2 whole, which is shorter than its diff:
```python
import functools

import jax
import jax.numpy as jnp
from jax import lax
from jax.experimental import pallas as pl
from jax.experimental.pallas import tpu as pltpu
from jax.sharding import PartitionSpec as P

MESH = pl.DeviceIdType.MESH
HDIM = 128
WIDTH = 256
LAMBDA_INIT = 0.8
EPSILON = 1e-05
MASKED = -1e30
SCALE = HDIM**-0.5
LOG2E = 1.4426950408889634
F32 = jnp.float32
BF16 = jnp.bfloat16


def mm(a, b, dims=((1,), (0,))):
    return lax.dot_general(a, b, (dims, ((), ())), preferred_element_type=F32)


NT = ((1,), (1,))
TN = ((0,), (0,))


def kernel(
    order, lam, gain, qh, kh, vh, og, wq, wk, wv, wo, out, zr,
    kb, vb, qb, gs, gb, ogb, wob, wb, st, pb, qt, d0, ot, gacc, gt, gn, dq,
    sibs, sibr, own, ys, yr, dqs, dks, rb, pa, xs_, xr, xf, zs,
    wsem, lsem, ssem, rsem,
):
    ctx = lax.axis_index("ctx")
    hd = lax.axis_index("heads")
    hi = lax.div(ctx, 8)
    y = lax.rem(lax.div(ctx, 2), 4)
    c = lax.rem(ctx, 2)
    lo = lax.div(hd, 4)
    x = lax.rem(hd, 4)

    def dev(hi_, y_, c_, lo_, x_):
        return (hi_ * 8 + y_ * 2 + c_, lo_ * 4 + x_)

    sib = dev(hi, y, 1 - c, lo, x)
    ydev = {s: dev(hi, lax.rem(y + s, 4), c, lo, x) for s in (1, 2, 3)}
    xdev = {s: dev(hi, y, c, lo, lax.rem(x + s, 4)) for s in (1, 2, 3)}
    far = dev(1 - hi, y, c, lo, x)
    partner = dev(hi, y, c, 1 - lo, x)

    barrier = pltpu.get_barrier_semaphore()
    others = [sib, far, partner, *ydev.values(), *xdev.values()]
    for d in others:
        pl.semaphore_signal(barrier, inc=1, device_id=d, device_id_type=MESH)

    def half(rel):
        head = hi if rel == 0 else 1 - hi
        return pl.ds(pl.multiple_of(head * 256, 256), 256)

    count = [0]

    def load(src, dst):
        cp = pltpu.make_async_copy(src, dst, lsem.at[count[0]])
        count[0] += 1
        cp.start()
        return cp

    own_k = load(kh.at[:, half(0)], kb.at[0, 0, 0])
    own_v = load(vh.at[:, half(0)], vb.at[0, 0, 0])
    own_q = load(qh.at[:, half(0)], qb.at[pl.ds(0, 128)])
    own_og = load(og, ogb.at[0, 0])
    wo_copies = {}
    for s in range(4):
        for r in range(2):
            block = lax.rem(lo + r, 2) * 4 + lax.rem(x + s, 4)
            at = pl.ds(pl.multiple_of(block * 512, 512), 512)
            wo_copies[r, s] = load(wo.at[:, at], wob.at[r, s])
    w_copies = []
    for k, w in enumerate((wq, wk, wv)):
        for rel in range(2):
            w_copies.append(load(w.at[:, half(rel)], wb.at[k, :, pl.ds(rel * 256, 256)]))

    pl.semaphore_wait(barrier, len(others))

    used = [0]
    sent = []
    names = {}

    def num(*key):
        if key not in names:
            names[key] = len(names)
        return names[key]

    def send(src, dst, key, to):
        n = used[0]
        used[0] += 1
        cp = pltpu.make_async_remote_copy(
            src_ref=src, dst_ref=dst, send_sem=ssem.at[n], recv_sem=rsem.at[num(*key)],
            device_id=to, device_id_type=MESH,
        )
        cp.start()
        sent.append(cp)

    def arrived(dst, *key):
        pltpu.make_async_remote_copy(
            src_ref=dst, dst_ref=dst, send_sem=ssem.at[0], recv_sem=rsem.at[num(*key)],
            device_id=sib, device_id_type=MESH,
        ).wait_recv()

    def gather_y(src, buf, kind, t):
        for s in (3, 1, 2):
            send(src, buf.at[s, 0, t], (kind, s, 0, t), ydev[4 - s])

    def twin(buf, kind, s, t):
        send(buf.at[s, 0, t], buf.at[s, 1, t], (kind, s, 1, t), sib)

    def gather_x(src, r):
        for s in (3, 1, 2):
            send(src, ogb.at[r, s], ("og", r, s), xdev[4 - s])

    gather_y(kh.at[:, half(0)], kb, "k", 0)
    send(og, ogb.at[1, 0], ("og", 1, 0), partner)
    send(kh.at[:, half(1)], kb.at[0, 0, 1], ("k", 0, 0, 1), far)
    gather_x(og, 0)
    send(kh.at[:, half(0)], kb.at[0, 1, 0], ("k", 0, 1, 0), sib)
    gather_y(vh.at[:, half(0)], vb, "v", 0)
    send(vh.at[:, half(1)], vb.at[0, 0, 1], ("v", 0, 0, 1), far)
    send(qh.at[:, half(1)], qb.at[pl.ds(128, 128)], ("q",), far)
    send(vh.at[:, half(0)], vb.at[0, 1, 0], ("v", 0, 1, 0), sib)

    lane = lax.broadcasted_iota(jnp.int32, (64, 256), 1)
    row = lax.broadcasted_iota(jnp.int32, (64, 256), 0)

    def stretch(s, r, t, piece):
        token_half = hi if t == 0 else 1 - hi
        block = token_half * 8 + lax.rem(y + s, 4) * 2 + lax.rem(c + r, 2)
        return order[block * 2 + piece]

    qs = [stretch(0, 0, t, piece) for t in range(2) for piece in range(2)]
    qstretch = jnp.where(
        lane < 128,
        jnp.where(lane < 64, qs[0], qs[1]),
        jnp.where(lane < 192, qs[2], qs[3]),
    )
    d0[...] = row - qstretch * 64 - lax.rem(lane, 64)

    def scores(s, r, t, peak):
        i = (s * 2 + r) * 2 + t
        peaks = list(peak)
        for j in range(2):
            sc = mm(kb[s, r, t, :, j * 128 : j * 128 + 128], qt[j]) * (SCALE * LOG2E)
            for n in range(2):
                threshold = stretch(s, r, t, n) * -64
                part = jnp.where(d0[...] <= threshold, sc[n * 64 : n * 64 + 64], MASKED)
                st[j, i, n * 64 : n * 64 + 64] = part
                peaks[j] = jnp.maximum(peaks[j], jnp.max(part.reshape(8, 8, 256), axis=0))
        return tuple(peaks)

    def gdot(r, s, start=False):
        wo_copies[r, s].wait()
        term = mm(wob[r, s], ogb[r, s], NT)
        gacc[...] = term if start else gacc[...] + term

    arrived(kb.at[0, 0, 1], "k", 0, 0, 1)
    gather_y(kb.at[0, 0, 1], kb, "k", 1)
    twin(kb, "k", 0, 1)
    arrived(ogb.at[1, 0], "og", 1, 0)
    gather_x(ogb.at[1, 0], 1)
    arrived(vb.at[0, 0, 1], "v", 0, 0, 1)
    gather_y(vb.at[0, 0, 1], vb, "v", 1)
    twin(vb, "v", 0, 1)
    for s in (1, 3, 2):
        arrived(kb.at[s, 0, 0], "k", s, 0, 0)
        twin(kb, "k", s, 0)
    own_q.wait()
    arrived(qb.at[pl.ds(128, 128)], "q")
    for j in range(2):
        qt[j] = jnp.transpose(qb[:, j * 128 : j * 128 + 128].astype(F32)).astype(BF16)
    peak = (jnp.full((8, 256), MASKED, F32),) * 2
    own_k.wait()
    for s in (0, 1, 3, 2):
        peak = scores(s, 0, 0, peak)
    peak = scores(0, 0, 1, peak)
    for s in (1, 3, 2):
        arrived(vb.at[s, 0, 0], "v", s, 0, 0)
        twin(vb, "v", s, 0)
    own_og.wait()
    gdot(0, 0, True)
    gdot(1, 0)
    for s in (1, 3, 2):
        arrived(ogb.at[0, s], "og", 0, s)
        gdot(0, s)
    for s, t in ((0, 0), (0, 1), (1, 0), (3, 0), (2, 0)):
        arrived(kb.at[s, 1, t], "k", s, 1, t)
        peak = scores(s, 1, t, peak)
    for s in (1, 3, 2):
        arrived(kb.at[s, 0, 1], "k", s, 0, 1)
        twin(kb, "k", s, 1)
        peak = scores(s, 0, 1, peak)
    for s in (1, 3, 2):
        arrived(ogb.at[1, s], "og", 1, s)
        gdot(1, s)
    gs[...] = gacc[half(1)].astype(BF16)
    send(gs, gb.at[1], ("g",), far)
    gb[0] = gacc[half(0)].astype(BF16)
    for s in (1, 3):
        arrived(vb.at[s, 0, 1], "v", s, 0, 1)
        twin(vb, "v", s, 1)
    for s in (1, 3, 2):
        arrived(kb.at[s, 1, 1], "k", s, 1, 1)
        peak = scores(s, 1, 1, peak)

    tops = [jnp.max(p, axis=0, keepdims=True) for p in peak]

    def weigh(i, sums):
        sums = list(sums)
        for n in range(2):
            for j in range(2):
                p = jnp.exp2(st[j, 2 * i + n] - tops[j])
                st[j, 2 * i + n] = p
                sums[j] = sums[j] + jnp.sum(p.reshape(16, 8, 256), axis=0)
                pb[2 * i + n, :, j * 256 : j * 256 + 256] = p.astype(BF16)
        return tuple(sums)

    sums = lax.fori_loop(0, 8, weigh, (jnp.zeros((8, 256), F32),) * 2)
    inv = [1.0 / jnp.sum(p, axis=0, keepdims=True) for p in sums]

    def values(s, r):
        i = (s * 2 + r) * 2
        weights = pb[i : i + 2].reshape(256, 512)
        return mm(vb[s, r].reshape(256, 256), weights, TN)

    arrived(vb.at[2, 0, 1], "v", 2, 0, 1)
    twin(vb, "v", 2, 1)
    own_v.wait()
    ot[...] = values(0, 0)
    for s in (1, 3, 2):
        ot[...] += values(s, 0)
    for s in (0, 1, 3, 2):
        for t in range(2):
            arrived(vb.at[s, 1, t], "v", s, 1, t)
        ot[...] += values(s, 1)

    lam_own = lam[hi]
    gain_t = jnp.transpose(jnp.broadcast_to(gain[...], (128, 256)))
    gain_t = jnp.concatenate([gain_t, gain_t], axis=1)
    arrived(gb.at[1], "g")

    o1 = ot[:, :256] * inv[0]
    o2 = ot[:, 256:] * inv[1]
    combined = o1 - lam_own * o2
    rms = jnp.sqrt(jnp.mean(combined * combined, axis=0, keepdims=True) + EPSILON)
    inv_rms = 1.0 / rms
    normed = combined * inv_rms
    g = jnp.concatenate([gb[0], gb[1]], axis=1).astype(F32) * (gain_t * (1.0 - LAMBDA_INIT))
    grad = ((g - normed * jnp.mean(g * normed, axis=0, keepdims=True)) * inv_rms).astype(BF16)
    gt[...] = grad
    grad32 = grad.astype(F32)
    gn[...] = jnp.transpose(grad32).astype(BF16)
    stat1 = jnp.sum(grad32 * (ot[:, :256] * inv[0]), axis=0, keepdims=True)
    stat2 = jnp.sum(grad32 * (ot[:, 256:] * inv[1]), axis=0, keepdims=True)
    inv1 = inv[0]
    inv2 = inv[1] * lam_own

    dq[...] = jnp.zeros_like(dq)

    def backward(s, r, t):
        i = (s * 2 + r) * 2 + t
        dp = mm(vb[s, r, t], gt[...])
        p1 = st[0, i] * inv1
        p2 = st[1, i] * inv2
        mixed = (p1 - p2).astype(BF16)
        ds1 = (p1 * (dp - stat1)).astype(BF16)
        ds2 = (p2 * (dp - stat2)).astype(BF16)
        dv = mm(mixed, gn[...])
        dk1 = mm(ds1, qb[:, 0:128]) * SCALE
        dk2 = mm(ds2, qb[:, 128:256]) * -SCALE
        dq[0] += mm(kb[s, r, t, :, 0:128], ds1, TN)
        dq[1] += mm(kb[s, r, t, :, 128:256], ds2, TN)
        for part, at in ((dk1, 0), (dk2, 128), (dv, 256)):
            cols = pl.ds(at, part.shape[1])
            if r:
                sibs[t, s, :, cols] = part.astype(BF16)
            else:
                own[t, s, :, cols] = part
        if r:
            send(sibs.at[t, s], sibr.at[t, s], ("sib", t, s), sib)

    left, right = pl.ds(0, 256), pl.ds(256, 256)

    def total(t, s, cols):
        return own[t, s, :, cols] + sibr[t, s, :, cols].astype(F32)

    def chip_sum(t, s, cols):
        ys[t, s, :, cols] = total(t, s, cols).astype(BF16)

    def pass_on(t, s, cols, key):
        send(ys.at[t, s, :, cols], yr.at[t, s, :, cols], ("yr", t, s, key), ydev[s])

    def first_hop(t, begun=False):
        if not begun:
            backward(2, 1, t)
        backward(1, 1, t)
        backward(3, 1, t)
        backward(2, 0, t)
        arrived(sibr.at[t, 2], "sib", t, 2)
        chip_sum(t, 2, pl.ds(0, 512))
        send(ys.at[t, 2, :, left], yr.at[t, 0, :, left], ("y2", t, 0), ydev[1])
        send(ys.at[t, 2, :, right], yr.at[t, 0, :, right], ("y2", t, 1), ydev[3])
        backward(1, 0, t)
        arrived(sibr.at[t, 1], "sib", t, 1)
        chip_sum(t, 1, right)
        pass_on(t, 1, right, 1)
        backward(3, 0, t)
        arrived(sibr.at[t, 3], "sib", t, 3)
        chip_sum(t, 3, left)
        pass_on(t, 3, left, 0)
        backward(0, 1, t)
        backward(0, 0, t)

    def second_hop(t):
        arrived(yr.at[t, 0, :, left], "y2", t, 0)
        ys[t, 1, :, left] = (total(t, 1, left) + yr[t, 0, :, left].astype(F32)).astype(BF16)
        pass_on(t, 1, left, 0)
        arrived(yr.at[t, 0, :, right], "y2", t, 1)
        ys[t, 3, :, right] = (total(t, 3, right) + yr[t, 0, :, right].astype(F32)).astype(BF16)
        pass_on(t, 3, right, 1)

    def finish(t):
        arrived(sibr.at[t, 0], "sib", t, 0)
        arrived(yr.at[t, 3, :, left], "yr", t, 3, 0)
        arrived(yr.at[t, 1, :, right], "yr", t, 1, 1)
        arrived(yr.at[t, 1, :, left], "yr", t, 1, 0)
        arrived(yr.at[t, 3, :, right], "yr", t, 3, 1)
        whole = total(t, 0, pl.ds(0, 512)) + (yr[t, 1].astype(F32) + yr[t, 3].astype(F32))
        return jnp.transpose(whole).astype(BF16)

    first_hop(1)
    backward(2, 1, 0)
    second_hop(1)
    first_hop(0, True)
    for j, sign in ((0, SCALE), (1, -SCALE)):
        rb[0, 0, j * 128 : j * 128 + 128] = (dq[j, :, 0:128] * sign).astype(BF16)
        dqs[j * 128 : j * 128 + 128] = (dq[j, :, 128:256] * sign).astype(BF16)
    send(dqs, rb.at[0, 1], ("dq",), far)
    dks[...] = finish(1)
    send(dks.at[pl.ds(0, 256)], rb.at[1, 1], ("dk",), far)
    send(dks.at[pl.ds(256, 256)], rb.at[2, 1], ("dv",), far)
    second_hop(0)

    blocks = [(1, 2), (0, 2), (1, 3), (1, 1), (0, 1), (0, 3), (1, 0), (0, 0)]

    def rows(r, s):
        block = lax.rem(lo + r, 2) * 4 + lax.rem(x + s, 4)
        return pl.ds(pl.multiple_of(block * 512, 512), 512)

    for cp in w_copies:
        cp.wait()
    arrived(rb.at[0, 1], "dq")
    for r, s in blocks:
        pa[r, s] = mm(wb[0, rows(r, s)], rb[0].reshape(512, 128))
    mine = finish(0)
    rb[1, 0] = mine[:256]
    rb[2, 0] = mine[256:]
    arrived(rb.at[1, 1], "dk")
    arrived(rb.at[2, 1], "dv")

    def project(r, s):
        return (
            pa[r, s]
            + mm(wb[1, rows(r, s)], rb[1].reshape(512, 128))
            + mm(wb[2, rows(r, s)], rb[2].reshape(512, 128))
        )

    xs_[1, 1] = project(1, 2).astype(BF16)
    send(xs_.at[1, 1], xr.at[1], ("xr", 1), xdev[1])
    xs_[0, 1] = project(0, 2).astype(BF16)
    send(xs_.at[0, 1], xr.at[0], ("xr", 0), xdev[3])
    xs_[1, 2] = project(1, 3).astype(BF16)
    send(xs_.at[1, 2], xf.at[1, 1], ("xf", 1, 1), xdev[3])
    pa[1, 1] = project(1, 1)
    xs_[0, 0] = project(0, 1).astype(BF16)
    pa[0, 3] = project(0, 3)
    arrived(xr.at[1], "xr", 1)
    xs_[1, 0] = (pa[1, 1] + xr[1].astype(F32)).astype(BF16)
    send(xs_.at[1, 0], xf.at[0, 1], ("xf", 0, 1), xdev[1])
    send(xs_.at[0, 0], xf.at[0, 0], ("xf", 0, 0), xdev[1])
    arrived(xr.at[0], "xr", 0)
    xs_[0, 2] = (pa[0, 3] + xr[0].astype(F32)).astype(BF16)
    send(xs_.at[0, 2], xf.at[1, 0], ("xf", 1, 0), xdev[3])
    pa[1, 0] = project(1, 0)
    pa[0, 0] = project(0, 0)
    arrived(xf.at[1, 1], "xf", 1, 1)
    arrived(xf.at[0, 1], "xf", 0, 1)
    zs[...] = (pa[1, 0] + xf[0, 1].astype(F32) + xf[1, 1].astype(F32)).astype(BF16)
    send(zs, zr, ("zr",), partner)
    arrived(xf.at[0, 0], "xf", 0, 0)
    arrived(xf.at[1, 0], "xf", 1, 0)
    out[...] = pa[0, 0] + xf[0, 0].astype(F32) + xf[1, 0].astype(F32)
    arrived(zr, "zr")

    for cp in sent:
        cp.wait_send()


def body(order, qh, kh, vh, og, wq, wk, wv, wo, lam, gain):
    any_ = pl.BlockSpec(memory_space=pl.ANY)
    smem = pl.BlockSpec(memory_space=pltpu.SMEM)
    vmem = pl.BlockSpec(memory_space=pltpu.VMEM)
    v = pltpu.VMEM
    parts = pl.pallas_call(
        kernel,
        out_shape=(
            jax.ShapeDtypeStruct((512, 128), F32),
            jax.ShapeDtypeStruct((512, 128), BF16),
        ),
        in_specs=[smem, smem, vmem] + [any_] * 8,
        out_specs=(vmem, any_),
        scratch_shapes=[
            v((4, 2, 2, 128, 256), BF16),
            v((4, 2, 2, 128, 256), BF16),
            v((256, 256), BF16),
            v((256, 128), BF16),
            v((2, 256, 128), BF16),
            v((2, 4, 128, 512), BF16),
            v((2, 4, 512, 512), BF16),
            v((3, 4096, 512), BF16),
            v((2, 16, 128, 256), F32),
            v((16, 128, 512), BF16),
            v((2, 128, 256), BF16),
            v((64, 256), jnp.int32),
            v((256, 512), F32),
            v((512, 128), F32),
            v((256, 256), BF16),
            v((256, 256), BF16),
            v((2, 128, 256), F32),
            v((2, 4, 128, 512), BF16),
            v((2, 4, 128, 512), BF16),
            v((2, 4, 128, 512), F32),
            v((2, 4, 128, 512), BF16),
            v((2, 4, 128, 512), BF16),
            v((256, 128), BF16),
            v((512, 128), BF16),
            v((3, 2, 256, 128), BF16),
            v((2, 4, 512, 128), F32),
            v((2, 3, 512, 128), BF16),
            v((2, 512, 128), BF16),
            v((2, 2, 512, 128), BF16),
            v((512, 128), BF16),
            pltpu.SemaphoreType.DMA((1,)),
            pltpu.SemaphoreType.DMA((18,)),
            pltpu.SemaphoreType.DMA((96,)),
            pltpu.SemaphoreType.DMA((96,)),
        ],
        compiler_params=pltpu.CompilerParams(
            collective_id=0, has_side_effects=True, vmem_limit_bytes=56 * 2**20
        ),
        name="differential_attention_backward",
    )(order, lam, gain.reshape(1, 256), qh, kh, vh, og, wq, wk, wv, wo)
    return parts[0] + parts[1].astype(F32)


def solution(mesh):
    in_specs = (
        P(),
        P("ctx", "heads"),
        P("ctx", "heads"),
        P("ctx", "heads"),
        P("ctx", "heads"),
        P(None, "heads"),
        P(None, "heads"),
        P(None, "heads"),
        P("heads", None),
        P("heads"),
        P(),
    )
    out_specs = P("heads", "ctx")
    return jax.shard_map(body, mesh=mesh, in_specs=in_specs, out_specs=out_specs, check_vma=False)
```

time: 65.4 us -> 60.8 us (0.930)
  Pallas kernels: 63 us -> 58.9 us
  other arithmetic: 0 us -> 1.71 us
  local copies, waits for them, and re-layouts: 1.67 us -> 0 us
    pallas_call x1, Pallas kernels: 63 us -> 58.9 us  [body(): pl.pallas_call(kernel, out_shape=(jax.ShapeDtypeStruct((512, 128), F32),...]
    add x0 -> x1, other arithmetic: none -> 1.71 us  [body(): return parts[0] + parts[1].astype(F32)]
    unnamed x1 -> x0, local copies, waits for them, and re-layouts: 1.67 us -> none
where the time goes in v2:
time: 60.8 us; the launch traced here: 60.7 us
  Pallas kernels  58.9 us (97%)
  other arithmetic  1.71 us (3%)
    pallas_call x1, Pallas kernels, body(): pl.pallas_call(kernel, out_shape=(jax.ShapeDtypeStruct((512, 128), F32),...  58.9 us
    add x1, other arithmetic, body(): return parts[0] + parts[1].astype(F32)  1.71 us

profile of v2, /device:TPU:0, one launch (start us, length us, event | category | flops | bytes accessed | tf_op | source)
XLA Modules:
  0.0 60.7 jit_solution(3404070466887155705)
XLA Ops:
  0.0 58.9 %differential_attention_backward.1 = (f32[512,128]{1,0:T(8,128)}, bf16[512,128]{1,0:T(8,128)(2,1)}) custom-call(s32[32]{0:T(128)} %order.1, f32[2]{0:T(128)} %lam.1, f32[1,256]{1,0:T(1,128)} %bitcast.1, bf16[128,512]{1,0:T(8,128)(2,1)} %qh.1, bf16[128,512]{1,0:T(8,128)(2,1)} %kh.1, bf16[128,512]{1,0:T(8,128)(2,1)} %vh.1, bf16[128,512]{1,0:T(8,128)(2,1)} %og.1, ...), custom_call_target="tpu_custom_call" | custom-call | tf_op jit(solution)/shard_map/differential_attention_backward/pallas_call | solution.py:413
  58.9 1.7 %convert_add_fusion = f32[512,128]{1,0:T(8,128)} fusion(f32[512,128]{1,0:T(8,128)} %get-tuple-element.7, bf16[512,128]{1,0:T(8,128)(2,1)} %get-tuple-element.8), kind=kLoop, calls=%fused_computation | loop fusion | flops 131072 | bytes 655360 | tf_op jit(solution)/shard_map/add | solution.py:462

commit v3 on v2

v3 whole, which is shorter than its diff:
```python
import math

import jax
import jax.numpy as jnp
from jax import lax
from jax.experimental import pallas as pl
from jax.experimental.pallas import tpu as pltpu
from jax.sharding import PartitionSpec as P

MESH = pl.DeviceIdType.MESH
HDIM = 128
WIDTH = 256
LAMBDA_INIT = 0.8
EPSILON = 1e-05
MASKED = -1e30
SCALE = HDIM**-0.5
LOG2E = 1.4426950408889634
F32 = jnp.float32
BF16 = jnp.bfloat16


def mm(a, b, dims=((1,), (0,))):
    return lax.dot_general(a, b, (dims, ((), ())), preferred_element_type=F32)


RECEIVES = 91
LOADS = 22
NT = ((1,), (1,))
TN = ((0,), (0,))


def kernel(
    order_in, lam_in, gain_in, qh, kh, vh, og, wq, wk, wv, wo, out, zr,
    order, lam, gain, kb, vb, qb, gs, gb, ogb, wob, wb, st, pb, qt, d0, ot, gacc, gt, gn, dq,
    sibs, sibr, own, ys, yr, dqs, dks, rb, pa, xs_, xr, xf, zs, ob,
    lsem, ssem, rsem,
):
    ctx = lax.axis_index("ctx")
    hd = lax.axis_index("heads")
    hi = lax.div(ctx, 8)
    y = lax.rem(lax.div(ctx, 2), 4)
    c = lax.rem(ctx, 2)
    lo = lax.div(hd, 4)
    x = lax.rem(hd, 4)

    def dev(hi_, y_, c_, lo_, x_):
        return (hi_ * 8 + y_ * 2 + c_, lo_ * 4 + x_)

    sib = dev(hi, y, 1 - c, lo, x)
    ydev = {s: dev(hi, lax.rem(y + s, 4), c, lo, x) for s in (1, 2, 3)}
    xdev = {s: dev(hi, y, c, lo, lax.rem(x + s, 4)) for s in (1, 2, 3)}
    far = dev(1 - hi, y, c, lo, x)
    partner = dev(hi, y, c, 1 - lo, x)

    barrier = pltpu.get_barrier_semaphore()
    others = [sib, far, partner, *ydev.values(), *xdev.values()]
    for d in others:
        pl.semaphore_signal(barrier, inc=1, device_id=d, device_id_type=MESH)

    def half(rel):
        head = hi if rel == 0 else 1 - hi
        return pl.ds(pl.multiple_of(head * 256, 256), 256)

    count = [0]

    def load(src, dst):
        cp = pltpu.make_async_copy(src, dst, lsem.at[count[0]])
        count[0] += 1
        cp.start()
        return cp

    small = [load(order_in, order), load(lam_in, lam), load(gain_in, gain)]
    own_k = load(kh.at[:, half(0)], kb.at[0, 0, 0])
    own_v = load(vh.at[:, half(0)], vb.at[0, 0, 0])
    own_q = load(qh.at[:, half(0)], qb.at[pl.ds(0, 128)])
    own_og = load(og, ogb.at[0, 0])
    wo_copies = {}
    for s in range(4):
        for r in range(2):
            block = lax.rem(lo + r, 2) * 4 + lax.rem(x + s, 4)
            at = pl.ds(pl.multiple_of(block * 512, 512), 512)
            wo_copies[r, s] = load(wo.at[:, at], wob.at[r, s])
    w_copies = []
    for w, rel, group, at in (
        (wq, 0, 0, 0), (wq, 1, 0, 256), (wk, 0, 1, 0), (wv, 0, 1, 256), (wk, 1, 2, 0), (wv, 1, 2, 256),
    ):
        w_copies.append(load(w.at[:, half(rel)], wb.at[group, :, pl.ds(at, 256)]))

    pl.semaphore_wait(barrier, len(others))

    names = {}
    sent = [0]

    def num(*key):
        if key not in names:
            names[key] = len(names)
        return names[key]

    def send(src, dst, key, to):
        pltpu.make_async_remote_copy(
            src_ref=src, dst_ref=dst, send_sem=ssem.at[0], recv_sem=rsem.at[num(*key)],
            device_id=to, device_id_type=MESH,
        ).start()
        sent[0] += math.prod(src.shape) * src.dtype.itemsize

    def all_sent():
        rows = wb.at[0, pl.ds(0, sent[0] // 1024)]
        pltpu.make_async_remote_copy(
            src_ref=rows, dst_ref=rows, send_sem=ssem.at[0], recv_sem=rsem.at[0],
            device_id=sib, device_id_type=MESH,
        ).wait_send()
        sent[0] = 0

    def arrived(dst, *key):
        pltpu.make_async_remote_copy(
            src_ref=dst, dst_ref=dst, send_sem=ssem.at[0], recv_sem=rsem.at[num(*key)],
            device_id=sib, device_id_type=MESH,
        ).wait_recv()

    def gather_y(src, buf, kind, t, steps=(2, 3, 1)):
        for s in steps:
            send(src, buf.at[t, s, 0], (kind, s, 0, t), ydev[4 - s])

    def twin(buf, kind, s, t):
        send(buf.at[t, s, 0], buf.at[t, s, 1], (kind, s, 1, t), sib)

    def gather_x(src, r, steps=(2, 3, 1)):
        for s in steps:
            send(src, ogb.at[r, s], ("og", r, s), xdev[4 - s])

    send(kh.at[:, half(1)], kb.at[1, 0, 0], ("k", 0, 0, 1), far)
    send(og, ogb.at[1, 0], ("og", 1, 0), partner)
    gather_y(kh.at[:, half(0)], kb, "k", 0)
    gather_x(og, 0)
    send(vh.at[:, half(1)], vb.at[1, 0, 0], ("v", 0, 0, 1), far)
    gather_y(vh.at[:, half(0)], vb, "v", 0, (3, 1))
    send(qh.at[:, half(1)], qb.at[pl.ds(128, 128)], ("q",), far)
    send(kh.at[:, half(0)], kb.at[0, 0, 1], ("k", 0, 1, 0), sib)
    send(vh.at[:, half(0)], vb.at[0, 0, 1], ("v", 0, 1, 0), sib)

    for cp in small:
        cp.wait()
    lane = lax.broadcasted_iota(jnp.int32, (64, 256), 1)
    row = lax.broadcasted_iota(jnp.int32, (64, 256), 0)

    def stretch(s, r, t, piece):
        token_half = hi if t == 0 else 1 - hi
        block = token_half * 8 + lax.rem(y + s, 4) * 2 + lax.rem(c + r, 2)
        return order[block * 2 + piece]

    qs = [stretch(0, 0, t, piece) for t in range(2) for piece in range(2)]
    qstretch = jnp.where(
        lane < 128,
        jnp.where(lane < 64, qs[0], qs[1]),
        jnp.where(lane < 192, qs[2], qs[3]),
    )
    d0[...] = row - qstretch * 64 - lax.rem(lane, 64)

    def scores(s, r, t, peak):
        i = s * 2 + r
        peaks = list(peak)
        for j in range(2):
            sc = mm(kb[t, s, r, :, j * 128 : j * 128 + 128], qt[j]) * (SCALE * LOG2E)
            for n in range(2):
                threshold = stretch(s, r, t, n) * -64
                part = jnp.where(d0[...] <= threshold, sc[n * 64 : n * 64 + 64], MASKED)
                st[j, t, i, n * 64 : n * 64 + 64] = part
                peaks[j] = jnp.maximum(peaks[j], jnp.max(part.reshape(8, 8, 256), axis=0))
        return tuple(peaks)

    def gdot(r, s, start=False):
        wo_copies[r, s].wait()
        term = mm(wob[r, s], ogb[r, s], NT)
        gacc[...] = term if start else gacc[...] + term

    arrived(kb.at[1, 0, 0], "k", 0, 0, 1)
    gather_y(kb.at[1, 0, 0], kb, "k", 1)
    twin(kb, "k", 0, 1)
    arrived(ogb.at[1, 0], "og", 1, 0)
    gather_x(ogb.at[1, 0], 1, (3, 1))
    arrived(ogb.at[0, 2], "og", 0, 2)
    send(ogb.at[0, 2], ogb.at[1, 2], ("og", 1, 2), partner)
    for s in (1, 3, 2):
        arrived(kb.at[0, s, 0], "k", s, 0, 0)
        twin(kb, "k", s, 0)
    lower, upper = pl.ds(0, 64), pl.ds(64, 64)
    for s, part, to in ((3, lower, 1), (1, upper, 3)):
        arrived(vb.at[0, s, 0], "v", s, 0, 0)
        send(vb.at[0, s, 0, part], vb.at[0, 2, 0, part], ("v", 2, 0, 0, s), ydev[to])
        twin(vb, "v", s, 0)
    own_og.wait()
    gdot(0, 0, True)
    gdot(1, 0)
    gdot(0, 2)
    arrived(vb.at[1, 0, 0], "v", 0, 0, 1)
    gather_y(vb.at[1, 0, 0], vb, "v", 1)
    twin(vb, "v", 0, 1)
    for s in (1, 3):
        arrived(ogb.at[0, s], "og", 0, s)
        gdot(0, s)
    own_q.wait()
    arrived(qb.at[pl.ds(128, 128)], "q")
    for j in range(2):
        qt[j] = jnp.transpose(qb[:, j * 128 : j * 128 + 128].astype(F32)).astype(BF16)
    peak = (jnp.full((8, 256), MASKED, F32),) * 2
    own_k.wait()
    for s in (0, 1, 3, 2):
        peak = scores(s, 0, 0, peak)
    for s in (1, 3, 2):
        arrived(kb.at[1, s, 0], "k", s, 0, 1)
        twin(kb, "k", s, 1)
    for s in (1, 3, 2):
        arrived(ogb.at[1, s], "og", 1, s)
        gdot(1, s)
    gs[...] = gacc[half(1)].astype(BF16)
    send(gs, gb.at[1], ("g",), far)
    gb[0] = gacc[half(0)].astype(BF16)
    for s, part in ((3, lower), (1, upper)):
        arrived(vb.at[0, 2, 0, part], "v", 2, 0, 0, s)
    twin(vb, "v", 2, 0)
    for s in (0, 1, 3, 2):
        peak = scores(s, 0, 1, peak)
    for s in (0, 1, 3, 2):
        arrived(kb.at[0, s, 1], "k", s, 1, 0)
        peak = scores(s, 1, 0, peak)
    for s in (1, 3):
        arrived(vb.at[1, s, 0], "v", s, 0, 1)
        twin(vb, "v", s, 1)
    for s in (0, 1, 3, 2):
        arrived(kb.at[1, s, 1], "k", s, 1, 1)
        peak = scores(s, 1, 1, peak)

    tops = [jnp.max(p, axis=0, keepdims=True) for p in peak]

    def weigh(i, sums):
        sums = list(sums)
        for t in range(2):
            for j in range(2):
                p = jnp.exp2(st[j, t, i] - tops[j])
                st[j, t, i] = p
                sums[j] = sums[j] + jnp.sum(p.reshape(16, 8, 256), axis=0)
                pb[t, i, :, j * 256 : j * 256 + 256] = p.astype(BF16)
        return tuple(sums)

    sums = lax.fori_loop(0, 8, weigh, (jnp.zeros((8, 256), F32),) * 2)
    inv = [1.0 / jnp.sum(p, axis=0, keepdims=True) for p in sums]

    def values(t, s):
        return mm(vb[t, s].reshape(256, 256), pb[t, 2 * s : 2 * s + 2].reshape(256, 512), TN)

    arrived(vb.at[1, 2, 0], "v", 2, 0, 1)
    twin(vb, "v", 2, 1)
    own_v.wait()
    for s in (0, 1, 3, 2):
        arrived(vb.at[0, s, 1], "v", s, 1, 0)
    ot[...] = mm(vb[0].reshape(1024, 256), pb[0].reshape(1024, 512), TN)
    for s in (0, 1, 3, 2):
        arrived(vb.at[1, s, 1], "v", s, 1, 1)
        ot[...] += values(1, s)

    lam_own = lam[hi]
    gain_t = jnp.transpose(jnp.broadcast_to(gain[...], (128, 256)))
    gain_t = jnp.concatenate([gain_t, gain_t], axis=1)
    arrived(gb.at[1], "g")

    o1 = ot[:, :256] * inv[0]
    o2 = ot[:, 256:] * inv[1]
    combined = o1 - lam_own * o2
    rms = jnp.sqrt(jnp.mean(combined * combined, axis=0, keepdims=True) + EPSILON)
    inv_rms = 1.0 / rms
    normed = combined * inv_rms
    g = jnp.concatenate([gb[0], gb[1]], axis=1).astype(F32) * (gain_t * (1.0 - LAMBDA_INIT))
    grad = ((g - normed * jnp.mean(g * normed, axis=0, keepdims=True)) * inv_rms).astype(BF16)
    gt[...] = grad
    grad32 = grad.astype(F32)
    gn[...] = jnp.transpose(grad32).astype(BF16)
    stat1 = jnp.sum(grad32 * (ot[:, :256] * inv[0]), axis=0, keepdims=True)
    stat2 = jnp.sum(grad32 * (ot[:, 256:] * inv[1]), axis=0, keepdims=True)
    inv1 = inv[0]
    inv2 = inv[1] * lam_own

    dq[...] = jnp.zeros_like(dq)

    def backward(s, r):
        i = s * 2 + r
        dp = mm(vb[:, s, r].reshape(256, 256), gt[...])
        keys = kb[:, s, r].reshape(256, 256)
        p1 = st[0, :, i].reshape(256, 256) * inv1
        p2 = st[1, :, i].reshape(256, 256) * inv2
        mixed = (p1 - p2).astype(BF16)
        ds1 = (p1 * (dp - stat1)).astype(BF16)
        ds2 = (p2 * (dp - stat2)).astype(BF16)
        dv = mm(mixed, gn[...])
        dk1 = mm(ds1, qb[:, 0:128]) * SCALE
        dk2 = mm(ds2, qb[:, 128:256]) * -SCALE
        dq[0] += mm(keys[:, 0:128], ds1, TN)
        dq[1] += mm(keys[:, 128:256], ds2, TN)
        for part, at in ((dk1, 0), (dk2, 128), (dv, 256)):
            cols = pl.ds(at, part.shape[1])
            for t in range(2):
                piece = part[t * 128 : t * 128 + 128]
                if r:
                    sibs[s, t, :, cols] = piece.astype(BF16)
                else:
                    own[t, s, :, cols] = piece
        if r:
            send(sibs.at[s], sibr.at[s], ("sib", s), sib)

    both = pl.ds(0, 512)
    ups = {0: [pl.ds(0, 256)], 1: [pl.ds(0, 128), pl.ds(128, 128)]}
    downs = {0: [pl.ds(256, 256)], 1: [pl.ds(256, 128), pl.ds(384, 128)]}

    def total(t, s, cols):
        return own[t, s, :, cols] + sibr[s, t, :, cols].astype(F32)

    def chip_sum(t, s, cols):
        ys[t, s, :, cols] = total(t, s, cols).astype(BF16)

    def pass_on(t, s, cols, *key):
        send(ys.at[t, s, :, cols], yr.at[t, s, :, cols], ("yr", t, s, *key), ydev[s])

    def first_hop(t):
        chip_sum(t, 2, both)
        for n, (up, down) in enumerate(zip(ups[t], downs[t])):
            send(ys.at[t, 2, :, up], yr.at[t, 0, :, up], ("y2", t, 0, n), ydev[1])
            send(ys.at[t, 2, :, down], yr.at[t, 0, :, down], ("y2", t, 1, n), ydev[3])

    def straight(t, s):
        cols = pl.ds(256, 256) if s == 1 else pl.ds(0, 256)
        chip_sum(t, s, cols)
        pass_on(t, s, cols, "direct")

    def second_hop(t):
        for n, (up, down) in enumerate(zip(ups[t], downs[t])):
            for s, cols, way in ((1, up, 0), (3, down, 1)):
                arrived(yr.at[t, 0, :, cols], "y2", t, way, n)
                ys[t, s, :, cols] = (total(t, s, cols) + yr[t, 0, :, cols].astype(F32)).astype(BF16)
                pass_on(t, s, cols, n)

    def finish(t, n, cols, s):
        arrived(yr.at[t, s, :, cols], "yr", t, s, n)
        whole = total(t, 0, cols) + (yr[t, 1, :, cols].astype(F32) + yr[t, 3, :, cols].astype(F32))
        return jnp.transpose(whole).astype(BF16)

    def finish_direct(t):
        arrived(yr.at[t, 3, :, pl.ds(0, 256)], "yr", t, 3, "direct")
        arrived(yr.at[t, 1, :, pl.ds(256, 256)], "yr", t, 1, "direct")

    all_sent()
    backward(2, 1)
    backward(2, 0)
    backward(1, 1)
    backward(3, 1)
    arrived(sibr.at[2], "sib", 2)
    first_hop(1)
    backward(1, 0)
    arrived(sibr.at[1], "sib", 1)
    straight(1, 1)
    backward(3, 0)
    arrived(sibr.at[3], "sib", 3)
    straight(1, 3)
    first_hop(0)
    backward(0, 1)
    backward(0, 0)
    for j, sign in ((0, SCALE), (1, -SCALE)):
        rb[0, j * 128 : j * 128 + 128] = (dq[j, :, 0:128] * sign).astype(BF16)
        dqs[j * 128 : j * 128 + 128] = (dq[j, :, 128:256] * sign).astype(BF16)
    send(dqs, rb.at[0, pl.ds(256, 256)], ("dq",), far)
    straight(0, 1)
    straight(0, 3)
    second_hop(1)
    arrived(sibr.at[0], "sib", 0)
    finish_direct(1)
    second_hop(0)
    for n, (up, down) in enumerate(zip(ups[1], downs[1])):
        for s, cols in ((1, up), (3, down)):
            dks[cols, :] = finish(1, n, cols, s)
            send(dks.at[cols], rb.at[2, cols], ("dk", n, s), far)

    blocks = [(1, 2), (1, 1), (1, 3), (0, 2), (0, 1), (0, 3), (1, 0), (0, 0)]

    def rows(r, s):
        block = lax.rem(lo + r, 2) * 4 + lax.rem(x + s, 4)
        return pl.ds(pl.multiple_of(block * 512, 512), 512)

    for cp in w_copies:
        cp.wait()
    arrived(rb.at[0, pl.ds(256, 256)], "dq")
    for r, s in blocks:
        pa[r, s] = mm(wb[0, rows(r, s)], rb[0])
    finish_direct(0)
    for s, cols in ((1, ups[0][0]), (3, downs[0][0])):
        rb[1, cols, :] = finish(0, 0, cols, s)
    early = blocks[:2]
    for r, s in early:
        pa[r, s] += mm(wb[1, rows(r, s)], rb[1])
    for n in range(2):
        for s, cols in ((1, ups[1][n]), (3, downs[1][n])):
            arrived(rb.at[2, cols], "dk", n, s)

    def project(r, s):
        near = 0 if (r, s) in early else mm(wb[1, rows(r, s)], rb[1])
        return pa[r, s] + (near + mm(wb[2, rows(r, s)], rb[2]))

    def tops_of(q):
        return pl.ds(q * 256, 128)

    def bottoms_of(q):
        return pl.ds(q * 256 + 128, 128)

    def x_first(r):
        xs_[r, 2] = project(r, 2).astype(BF16)
        for q in range(2):
            for part, way, to in ((tops_of(q), 0, 1), (bottoms_of(q), 1, 3)):
                send(xs_.at[r, 2, part], xr.at[r, part], ("xr", r, q, way), xdev[to])

    def x_pass(r, s, part, *key):
        send(xs_.at[r, s, part], xf.at[s // 2, r, part], ("xf", s, r, *key), xdev[s])

    def x_direct(r):
        for q in range(2):
            for s, part in ((1, bottoms_of(q)), (3, tops_of(q))):
                xs_[r, s, part] = pa[r, s, part].astype(BF16)
                x_pass(r, s, part, q, 0)

    def x_second(r, q):
        for s, part, way in ((1, tops_of(q), 0), (3, bottoms_of(q), 1)):
            arrived(xr.at[r, part], "xr", r, q, way)
            xs_[r, s, part] = (pa[r, s, part] + xr[r, part].astype(F32)).astype(BF16)
            x_pass(r, s, part, q, 1)

    def x_final(r, q):
        for s, part, n in (
            (1, bottoms_of(q), 0), (3, tops_of(q), 0), (1, tops_of(q), 1), (3, bottoms_of(q), 1),
        ):
            arrived(xf.at[s // 2, r, part], "xf", s, r, q, n)
        part = pl.ds(q * 256, 256)
        return pa[r, 0, part] + (xf[0, r, part].astype(F32) + xf[1, r, part].astype(F32))

    x_first(1)
    pa[1, 1] = project(1, 1)
    pa[1, 3] = project(1, 3)
    x_direct(1)
    x_first(0)
    for r, s in ((0, 1), (0, 3), (1, 0), (0, 0)):
        pa[r, s] = project(r, s)
    x_second(1, 0)
    x_second(1, 1)
    x_direct(0)
    x_second(0, 0)
    x_second(0, 1)
    for q in range(2):
        part = pl.ds(q * 256, 256)
        zs[part, :] = x_final(1, q).astype(BF16)
        send(zs.at[part], zr.at[part], ("zr", q), partner)
    for q in range(2):
        ob[pl.ds(q * 256, 256), :] = x_final(0, q)
    done = load(ob, out)
    all_sent()
    done.wait()
    for q in range(2):
        arrived(zr.at[pl.ds(q * 256, 256)], "zr", q)
    assert (len(names), count[0]) == (RECEIVES, LOADS), (len(names), count[0])


def body(order, qh, kh, vh, og, wq, wk, wv, wo, lam, gain):
    any_ = pl.BlockSpec(memory_space=pl.ANY)
    v = pltpu.VMEM
    parts = pl.pallas_call(
        kernel,
        out_shape=(
            jax.ShapeDtypeStruct((512, 128), F32),
            jax.ShapeDtypeStruct((512, 128), BF16),
        ),
        in_specs=[any_] * 11,
        out_specs=(any_, any_),
        scratch_shapes=[
            pltpu.SMEM((32,), jnp.int32),
            pltpu.SMEM((2,), F32),
            v((1, 256), F32),
            v((2, 4, 2, 128, 256), BF16),
            v((2, 4, 2, 128, 256), BF16),
            v((256, 256), BF16),
            v((256, 128), BF16),
            v((2, 256, 128), BF16),
            v((2, 4, 128, 512), BF16),
            v((2, 4, 512, 512), BF16),
            v((3, 4096, 512), BF16),
            v((2, 2, 8, 128, 256), F32),
            v((2, 8, 128, 512), BF16),
            v((2, 128, 256), BF16),
            v((64, 256), jnp.int32),
            v((256, 512), F32),
            v((512, 128), F32),
            v((256, 256), BF16),
            v((256, 256), BF16),
            v((2, 128, 256), F32),
            v((4, 2, 128, 512), BF16),
            v((4, 2, 128, 512), BF16),
            v((2, 4, 128, 512), F32),
            v((2, 4, 128, 512), BF16),
            v((2, 4, 128, 512), BF16),
            v((256, 128), BF16),
            v((512, 128), BF16),
            v((3, 512, 128), BF16),
            v((2, 4, 512, 128), F32),
            v((2, 4, 512, 128), BF16),
            v((2, 512, 128), BF16),
            v((2, 2, 512, 128), BF16),
            v((512, 128), BF16),
            v((512, 128), F32),
            pltpu.SemaphoreType.DMA((LOADS,)),
            pltpu.SemaphoreType.DMA((1,)),
            pltpu.SemaphoreType.DMA((RECEIVES,)),
        ],
        compiler_params=pltpu.CompilerParams(
            collective_id=0, has_side_effects=True, vmem_limit_bytes=56 * 2**20
        ),
        name="differential_attention_backward",
    )(order, lam, gain.reshape(1, 256), qh, kh, vh, og, wq, wk, wv, wo)
    return parts[0] + parts[1].astype(F32)


def solution(mesh):
    in_specs = (
        P(),
        P("ctx", "heads"),
        P("ctx", "heads"),
        P("ctx", "heads"),
        P("ctx", "heads"),
        P(None, "heads"),
        P(None, "heads"),
        P(None, "heads"),
        P("heads", None),
        P("heads"),
        P(),
    )
    out_specs = P("heads", "ctx")
    return jax.shard_map(body, mesh=mesh, in_specs=in_specs, out_specs=out_specs, check_vma=False)
```

time: 60.8 us -> 54.7 us (0.90)
  Pallas kernels: 58.9 us -> 52.7 us
    pallas_call x1, Pallas kernels: 58.9 us -> 52.7 us  [body(): pl.pallas_call(kernel, out_shape=(jax.ShapeDtypeStruct((512, 128), F32),...]
where the time goes in v3:
time: 54.7 us; the launch traced here: 54.4 us
  Pallas kernels  52.7 us (96%)
  other arithmetic  1.71 us (3%)
    pallas_call x1, Pallas kernels, body(): pl.pallas_call(kernel, out_shape=(jax.ShapeDtypeStruct((512, 128), F32),...  52.7 us
    add x1, other arithmetic, body(): return parts[0] + parts[1].astype(F32)  1.71 us

profile of v3, /device:TPU:0, one launch (start us, length us, event | category | flops | bytes accessed | tf_op | source)
XLA Modules:
  0.0 54.4 jit_solution(3066113330499551865)
XLA Ops:
  0.0 52.7 %differential_attention_backward.1 = (f32[512,128]{1,0:T(8,128)}, bf16[512,128]{1,0:T(8,128)(2,1)}) custom-call(s32[32]{0:T(128)} %order_in.1, f32[2]{0:T(128)} %lam_in.1, f32[1,256]{1,0:T(1,128)} %bitcast.1, bf16[128,512]{1,0:T(8,128)(2,1)} %qh.1, bf16[128,512]{1,0:T(8,128)(2,1)} %kh.1, bf16[128,512]{1,0:T(8,128)(2,1)} %vh.1, bf16[128,512]{1,0:T(8,128)(2,1)} %og.1, ...), custom_call_target="tpu_custom_call" | custom-call | tf_op jit(solution)/shard_map/differential_attention_backward/pallas_call | solution.py:469
  52.7 1.7 %convert_add_fusion = f32[512,128]{1,0:T(8,128)} fusion(f32[512,128]{1,0:T(8,128)} %get-tuple-element.7, bf16[512,128]{1,0:T(8,128)(2,1)} %get-tuple-element.8), kind=kLoop, calls=%fused_computation | loop fusion | flops 131072 | bytes 655360 | tf_op jit(solution)/shard_map/add | solution.py:521

commit v4 on v3

--- a/solution.py
+++ b/solution.py
@@ -23,8 +23,8 @@
     return lax.dot_general(a, b, (dims, ((), ())), preferred_element_type=F32)
 
 
-RECEIVES = 91
-LOADS = 22
+RECEIVES = 42
+LOADS = 7
 NT = ((1,), (1,))
 TN = ((0,), (0,))
 
@@ -61,30 +61,28 @@
         head = hi if rel == 0 else 1 - hi
         return pl.ds(pl.multiple_of(head * 256, 256), 256)
 
-    count = [0]
-
-    def load(src, dst):
-        cp = pltpu.make_async_copy(src, dst, lsem.at[count[0]])
-        count[0] += 1
+    def load(src, dst, n):
+        cp = pltpu.make_async_copy(src, dst, lsem.at[n])
         cp.start()
         return cp
 
-    small = [load(order_in, order), load(lam_in, lam), load(gain_in, gain)]
-    own_k = load(kh.at[:, half(0)], kb.at[0, 0, 0])
-    own_v = load(vh.at[:, half(0)], vb.at[0, 0, 0])
-    own_q = load(qh.at[:, half(0)], qb.at[pl.ds(0, 128)])
-    own_og = load(og, ogb.at[0, 0])
-    wo_copies = {}
+    small = [load(order_in, order, 0), load(lam_in, lam, 1), load(gain_in, gain, 2)]
+    load(kh.at[:, half(0)], kb.at[0, 0, 0], 3)
+    load(vh.at[:, half(0)], vb.at[0, 0, 0], 3)
+    load(qh.at[:, half(0)], qb.at[pl.ds(0, 128)], 3)
+    load(og, ogb.at[0, 0], 3)
     for s in range(4):
         for r in range(2):
             block = lax.rem(lo + r, 2) * 4 + lax.rem(x + s, 4)
             at = pl.ds(pl.multiple_of(block * 512, 512), 512)
-            wo_copies[r, s] = load(wo.at[:, at], wob.at[r, s])
-    w_copies = []
+            load(wo.at[:, at], wob.at[r, s], 4)
     for w, rel, group, at in (
         (wq, 0, 0, 0), (wq, 1, 0, 256), (wk, 0, 1, 0), (wv, 0, 1, 256), (wk, 1, 2, 0), (wv, 1, 2, 256),
     ):
-        w_copies.append(load(w.at[:, half(rel)], wb.at[group, :, pl.ds(at, 256)]))
+        load(w.at[:, half(rel)], wb.at[group, :, pl.ds(at, 256)], 5)
+
+    def loaded(ref, n):
+        pltpu.make_async_copy(ref, ref, lsem.at[n]).wait()
 
     pl.semaphore_wait(barrier, len(others))
 
@@ -117,26 +115,26 @@
             device_id=sib, device_id_type=MESH,
         ).wait_recv()
 
-    def gather_y(src, buf, kind, t, steps=(2, 3, 1)):
+    def gather_y(src, buf, key, t, steps=(2, 3, 1)):
         for s in steps:
-            send(src, buf.at[t, s, 0], (kind, s, 0, t), ydev[4 - s])
-
-    def twin(buf, kind, s, t):
-        send(buf.at[t, s, 0], buf.at[t, s, 1], (kind, s, 1, t), sib)
+            send(src, buf.at[t, s, 0], (*key, s) if len(key) > 1 else key, ydev[4 - s])
+
+    def twin(buf, s, t, *key):
+        send(buf.at[t, s, 0], buf.at[t, s, 1], key, sib)
 
     def gather_x(src, r, steps=(2, 3, 1)):
         for s in steps:
-            send(src, ogb.at[r, s], ("og", r, s), xdev[4 - s])
-
-    send(kh.at[:, half(1)], kb.at[1, 0, 0], ("k", 0, 0, 1), far)
-    send(og, ogb.at[1, 0], ("og", 1, 0), partner)
-    gather_y(kh.at[:, half(0)], kb, "k", 0)
+            send(src, ogb.at[r, s], ("og", r, s == 2), xdev[4 - s])
+
+    send(kh.at[:, half(1)], kb.at[1, 0, 0], ("k far",), far)
+    send(og, ogb.at[1, 0], ("og partner",), partner)
+    gather_y(kh.at[:, half(0)], kb, ("k0",), 0)
     gather_x(og, 0)
-    send(vh.at[:, half(1)], vb.at[1, 0, 0], ("v", 0, 0, 1), far)
-    gather_y(vh.at[:, half(0)], vb, "v", 0, (3, 1))
+    send(vh.at[:, half(1)], vb.at[1, 0, 0], ("v far",), far)
+    gather_y(vh.at[:, half(0)], vb, ("v0",), 0, (3, 1))
     send(qh.at[:, half(1)], qb.at[pl.ds(128, 128)], ("q",), far)
-    send(kh.at[:, half(0)], kb.at[0, 0, 1], ("k", 0, 1, 0), sib)
-    send(vh.at[:, half(0)], vb.at[0, 0, 1], ("v", 0, 1, 0), sib)
+    send(kh.at[:, half(0)], kb.at[0, 0, 1], ("k0 twin",), sib)
+    send(vh.at[:, half(0)], vb.at[0, 0, 1], ("v0 twin",), sib)
 
     for cp in small:
         cp.wait()
@@ -156,79 +154,79 @@
     )
     d0[...] = row - qstretch * 64 - lax.rem(lane, 64)
 
-    def scores(s, r, t, peak):
-        i = s * 2 + r
+    def scores(s, t, peak):
         peaks = list(peak)
         for j in range(2):
-            sc = mm(kb[t, s, r, :, j * 128 : j * 128 + 128], qt[j]) * (SCALE * LOG2E)
-            for n in range(2):
-                threshold = stretch(s, r, t, n) * -64
+            keys = kb[t, s].reshape(256, 256)[:, j * 128 : j * 128 + 128]
+            sc = mm(keys, qt[j]) * (SCALE * LOG2E)
+            for n in range(4):
+                threshold = stretch(s, n // 2, t, n % 2) * -64
                 part = jnp.where(d0[...] <= threshold, sc[n * 64 : n * 64 + 64], MASKED)
-                st[j, t, i, n * 64 : n * 64 + 64] = part
+                at = pl.ds(n % 2 * 64, 64)
+                st[j, t, s * 2 + n // 2, at] = part
                 peaks[j] = jnp.maximum(peaks[j], jnp.max(part.reshape(8, 8, 256), axis=0))
         return tuple(peaks)
 
-    def gdot(r, s, start=False):
-        wo_copies[r, s].wait()
-        term = mm(wob[r, s], ogb[r, s], NT)
-        gacc[...] = term if start else gacc[...] + term
-
-    arrived(kb.at[1, 0, 0], "k", 0, 0, 1)
-    gather_y(kb.at[1, 0, 0], kb, "k", 1)
-    twin(kb, "k", 0, 1)
-    arrived(ogb.at[1, 0], "og", 1, 0)
+    def gdot(r, s, head=None, start=False):
+        rows = pl.ds(0, 512) if head is None else half(head)
+        term = mm(wob[r, s, rows], ogb[r, s], NT)
+        gacc[rows] = term if start else gacc[rows] + term
+
+    arrived(kb.at[1, 0, 0], "k far")
+    gather_y(kb.at[1, 0, 0], kb, ("k1",), 1)
+    twin(kb, 0, 1, "k1 twin")
+    arrived(ogb.at[1, 0], "og partner")
     gather_x(ogb.at[1, 0], 1, (3, 1))
-    arrived(ogb.at[0, 2], "og", 0, 2)
-    send(ogb.at[0, 2], ogb.at[1, 2], ("og", 1, 2), partner)
+    arrived(ogb.at[0, 2], "og", 0, True)
+    send(ogb.at[0, 2], ogb.at[1, 2], ("og", 1, True), partner)
+    arrived(kb.at[0, pl.ds(1, 3), 0], "k0")
     for s in (1, 3, 2):
-        arrived(kb.at[0, s, 0], "k", s, 0, 0)
-        twin(kb, "k", s, 0)
+        twin(kb, s, 0, "k0 twin")
     lower, upper = pl.ds(0, 64), pl.ds(64, 64)
+    arrived(vb.at[0, pl.ds(1, 2), 0], "v0")
     for s, part, to in ((3, lower, 1), (1, upper, 3)):
-        arrived(vb.at[0, s, 0], "v", s, 0, 0)
-        send(vb.at[0, s, 0, part], vb.at[0, 2, 0, part], ("v", 2, 0, 0, s), ydev[to])
-        twin(vb, "v", s, 0)
-    own_og.wait()
-    gdot(0, 0, True)
+        send(vb.at[0, s, 0, part], vb.at[0, 2, 0, part], ("v0 relay",), ydev[to])
+        twin(vb, s, 0, "v0 twin")
+    loaded(wb.at[0, pl.ds(0, 320)], 3)
+    loaded(wob, 4)
+    gdot(0, 0, start=True)
     gdot(1, 0)
     gdot(0, 2)
-    arrived(vb.at[1, 0, 0], "v", 0, 0, 1)
-    gather_y(vb.at[1, 0, 0], vb, "v", 1)
-    twin(vb, "v", 0, 1)
-    for s in (1, 3):
-        arrived(ogb.at[0, s], "og", 0, s)
-        gdot(0, s)
-    own_q.wait()
+    arrived(vb.at[1, 0, 0], "v far")
+    gather_y(vb.at[1, 0, 0], vb, ("v1", "y"), 1)
+    twin(vb, 0, 1, "v1 twin", 0)
+    arrived(ogb.at[0, pl.ds(0, 2)], "og", 0, False)
+    gdot(0, 1)
+    gdot(0, 3)
     arrived(qb.at[pl.ds(128, 128)], "q")
     for j in range(2):
         qt[j] = jnp.transpose(qb[:, j * 128 : j * 128 + 128].astype(F32)).astype(BF16)
     peak = (jnp.full((8, 256), MASKED, F32),) * 2
-    own_k.wait()
-    for s in (0, 1, 3, 2):
-        peak = scores(s, 0, 0, peak)
+    arrived(kb.at[0, :, 1], "k0 twin")
+    for s in (0, 1):
+        peak = scores(s, 0, peak)
+    arrived(kb.at[1, pl.ds(1, 3), 0], "k1")
     for s in (1, 3, 2):
-        arrived(kb.at[1, s, 0], "k", s, 0, 1)
-        twin(kb, "k", s, 1)
+        twin(kb, s, 1, "k1 twin")
+    arrived(ogb.at[1, pl.ds(0, 2)], "og", 1, False)
+    arrived(ogb.at[1, 2], "og", 1, True)
     for s in (1, 3, 2):
-        arrived(ogb.at[1, s], "og", 1, s)
-        gdot(1, s)
+        gdot(1, s, 1)
     gs[...] = gacc[half(1)].astype(BF16)
     send(gs, gb.at[1], ("g",), far)
+    for s in (1, 3, 2):
+        gdot(1, s, 0)
     gb[0] = gacc[half(0)].astype(BF16)
-    for s, part in ((3, lower), (1, upper)):
-        arrived(vb.at[0, 2, 0, part], "v", 2, 0, 0, s)
-    twin(vb, "v", 2, 0)
-    for s in (0, 1, 3, 2):
-        peak = scores(s, 0, 1, peak)
-    for s in (0, 1, 3, 2):
-        arrived(kb.at[0, s, 1], "k", s, 1, 0)
-        peak = scores(s, 1, 0, peak)
+    arrived(vb.at[0, 2, 0], "v0 relay")
+    twin(vb, 2, 0, "v0 twin")
+    for s in (3, 2):
+        peak = scores(s, 0, peak)
     for s in (1, 3):
-        arrived(vb.at[1, s, 0], "v", s, 0, 1)
-        twin(vb, "v", s, 1)
-    for s in (0, 1, 3, 2):
-        arrived(kb.at[1, s, 1], "k", s, 1, 1)
-        peak = scores(s, 1, 1, peak)
+        arrived(vb.at[1, s, 0], "v1", "y", s)
+        twin(vb, s, 1, "v1 twin", 0)
+    arrived(kb.at[1, :, 1], "k1 twin")
+    for s in range(4):
+        peak = scores(s, 1, peak)
 
     tops = [jnp.max(p, axis=0, keepdims=True) for p in peak]
 
@@ -248,15 +246,15 @@
     def values(t, s):
         return mm(vb[t, s].reshape(256, 256), pb[t, 2 * s : 2 * s + 2].reshape(256, 512), TN)
 
-    arrived(vb.at[1, 2, 0], "v", 2, 0, 1)
-    twin(vb, "v", 2, 1)
-    own_v.wait()
-    for s in (0, 1, 3, 2):
-        arrived(vb.at[0, s, 1], "v", s, 1, 0)
+    arrived(vb.at[1, 2, 0], "v1", "y", 2)
+    twin(vb, 2, 1, "v1 twin", 1)
+    arrived(vb.at[0, :, 1], "v0 twin")
     ot[...] = mm(vb[0].reshape(1024, 256), pb[0].reshape(1024, 512), TN)
-    for s in (0, 1, 3, 2):
-        arrived(vb.at[1, s, 1], "v", s, 1, 1)
+    arrived(vb.at[1, pl.ds(0, 3), 1], "v1 twin", 0)
+    for s in (0, 1, 3):
         ot[...] += values(1, s)
+    arrived(vb.at[1, 2, 1], "v1 twin", 1)
+    ot[...] += values(1, 2)
 
     lam_own = lam[hi]
     gain_t = jnp.transpose(jnp.broadcast_to(gain[...], (128, 256)))
@@ -306,9 +304,7 @@
         if r:
             send(sibs.at[s], sibr.at[s], ("sib", s), sib)
 
-    both = pl.ds(0, 512)
-    ups = {0: [pl.ds(0, 256)], 1: [pl.ds(0, 128), pl.ds(128, 128)]}
-    downs = {0: [pl.ds(256, 256)], 1: [pl.ds(256, 128), pl.ds(384, 128)]}
+    left, right, both = pl.ds(0, 256), pl.ds(256, 256), pl.ds(0, 512)
 
     def total(t, s, cols):
         return own[t, s, :, cols] + sibr[s, t, :, cols].astype(F32)
@@ -317,65 +313,66 @@
         ys[t, s, :, cols] = total(t, s, cols).astype(BF16)
 
     def pass_on(t, s, cols, *key):
-        send(ys.at[t, s, :, cols], yr.at[t, s, :, cols], ("yr", t, s, *key), ydev[s])
-
-    def first_hop(t):
-        chip_sum(t, 2, both)
-        for n, (up, down) in enumerate(zip(ups[t], downs[t])):
-            send(ys.at[t, 2, :, up], yr.at[t, 0, :, up], ("y2", t, 0, n), ydev[1])
-            send(ys.at[t, 2, :, down], yr.at[t, 0, :, down], ("y2", t, 1, n), ydev[3])
-
-    def straight(t, s):
-        cols = pl.ds(256, 256) if s == 1 else pl.ds(0, 256)
+        send(ys.at[t, s, :, cols], yr.at[t, s, :, cols], ("yr", t, *key), ydev[s])
+
+    def straight(t, s, cols, *key):
         chip_sum(t, s, cols)
-        pass_on(t, s, cols, "direct")
-
-    def second_hop(t):
-        for n, (up, down) in enumerate(zip(ups[t], downs[t])):
-            for s, cols, way in ((1, up, 0), (3, down, 1)):
-                arrived(yr.at[t, 0, :, cols], "y2", t, way, n)
-                ys[t, s, :, cols] = (total(t, s, cols) + yr[t, 0, :, cols].astype(F32)).astype(BF16)
-                pass_on(t, s, cols, n)
-
-    def finish(t, n, cols, s):
-        arrived(yr.at[t, s, :, cols], "yr", t, s, n)
-        whole = total(t, 0, cols) + (yr[t, 1, :, cols].astype(F32) + yr[t, 3, :, cols].astype(F32))
-        return jnp.transpose(whole).astype(BF16)
-
-    def finish_direct(t):
-        arrived(yr.at[t, 3, :, pl.ds(0, 256)], "yr", t, 3, "direct")
-        arrived(yr.at[t, 1, :, pl.ds(256, 256)], "yr", t, 1, "direct")
+        pass_on(t, s, cols, *key)
 
     all_sent()
     backward(2, 1)
     backward(2, 0)
     backward(1, 1)
     backward(3, 1)
+    def halfway(t, up, down, *key):
+        send(ys.at[t, 2, :, up], yr.at[t, 0, :, up], ("halfway", t, *key), ydev[1])
+        send(ys.at[t, 2, :, down], yr.at[t, 0, :, down], ("halfway", t, *key), ydev[3])
+
+    def second_hop(t, up, down, n):
+        for s, cols in ((1, up), (3, down)):
+            ys[t, s, :, cols] = (total(t, s, cols) + yr[t, 0, :, cols].astype(F32)).astype(BF16)
+            pass_on(t, s, cols, n)
+
+    groups = [(pl.ds(q * 128, 128), pl.ds(256 + q * 128, 128)) for q in range(2)]
+    a_group = yr.at[1, 0, :, left]
+
     arrived(sibr.at[2], "sib", 2)
-    first_hop(1)
+    chip_sum(1, 2, both)
+    for q, (up, down) in enumerate(groups):
+        halfway(1, up, down, q)
     backward(1, 0)
     arrived(sibr.at[1], "sib", 1)
-    straight(1, 1)
+    straight(1, 1, right, 2)
     backward(3, 0)
     arrived(sibr.at[3], "sib", 3)
-    straight(1, 3)
-    first_hop(0)
+    straight(1, 3, left, 2)
+    chip_sum(0, 2, both)
+    halfway(0, left, right)
     backward(0, 1)
     backward(0, 0)
     for j, sign in ((0, SCALE), (1, -SCALE)):
         rb[0, j * 128 : j * 128 + 128] = (dq[j, :, 0:128] * sign).astype(BF16)
         dqs[j * 128 : j * 128 + 128] = (dq[j, :, 128:256] * sign).astype(BF16)
     send(dqs, rb.at[0, pl.ds(256, 256)], ("dq",), far)
-    straight(0, 1)
-    straight(0, 3)
-    second_hop(1)
+    for q, (up, down) in enumerate(groups):
+        arrived(a_group, "halfway", 1, q)
+        second_hop(1, up, down, q)
+    straight(0, 1, right, 0)
+    straight(0, 3, left, 0)
     arrived(sibr.at[0], "sib", 0)
-    finish_direct(1)
-    second_hop(0)
-    for n, (up, down) in enumerate(zip(ups[1], downs[1])):
-        for s, cols in ((1, up), (3, down)):
-            dks[cols, :] = finish(1, n, cols, s)
-            send(dks.at[cols], rb.at[2, cols], ("dk", n, s), far)
+
+    def finish(t, cols):
+        whole = total(t, 0, cols) + (yr[t, 1, :, cols].astype(F32) + yr[t, 3, :, cols].astype(F32))
+        return jnp.transpose(whole).astype(BF16)
+
+    arrived(yr.at[0, 0], "halfway", 0)
+    second_hop(0, left, right, 0)
+    arrived(yr.at[1, 0], "yr", 1, 2)
+    for q, group in enumerate(groups):
+        arrived(a_group, "yr", 1, q)
+        for cols in group:
+            dks[cols, :] = finish(1, cols)
+            send(dks.at[cols], rb.at[2, cols], ("dk",), far)
 
     blocks = [(1, 2), (1, 1), (1, 3), (0, 2), (0, 1), (0, 3), (1, 0), (0, 0)]
 
@@ -383,59 +380,48 @@
         block = lax.rem(lo + r, 2) * 4 + lax.rem(x + s, 4)
         return pl.ds(pl.multiple_of(block * 512, 512), 512)
 
-    for cp in w_copies:
-        cp.wait()
+    loaded(wb, 5)
     arrived(rb.at[0, pl.ds(256, 256)], "dq")
     for r, s in blocks:
         pa[r, s] = mm(wb[0, rows(r, s)], rb[0])
-    finish_direct(0)
-    for s, cols in ((1, ups[0][0]), (3, downs[0][0])):
-        rb[1, cols, :] = finish(0, 0, cols, s)
+    arrived(yr.at[0, pl.ds(0, 2)], "yr", 0, 0)
+    for cols in (left, right):
+        rb[1, cols, :] = finish(0, cols)
     early = blocks[:2]
     for r, s in early:
         pa[r, s] += mm(wb[1, rows(r, s)], rb[1])
-    for n in range(2):
-        for s, cols in ((1, ups[1][n]), (3, downs[1][n])):
-            arrived(rb.at[2, cols], "dk", n, s)
+    arrived(rb.at[2], "dk")
 
     def project(r, s):
         near = 0 if (r, s) in early else mm(wb[1, rows(r, s)], rb[1])
         return pa[r, s] + (near + mm(wb[2, rows(r, s)], rb[2]))
 
-    def tops_of(q):
+    def top(q):
         return pl.ds(q * 256, 128)
 
-    def bottoms_of(q):
+    def bottom(q):
         return pl.ds(q * 256 + 128, 128)
 
     def x_first(r):
         xs_[r, 2] = project(r, 2).astype(BF16)
         for q in range(2):
-            for part, way, to in ((tops_of(q), 0, 1), (bottoms_of(q), 1, 3)):
-                send(xs_.at[r, 2, part], xr.at[r, part], ("xr", r, q, way), xdev[to])
-
-    def x_pass(r, s, part, *key):
-        send(xs_.at[r, s, part], xf.at[s // 2, r, part], ("xf", s, r, *key), xdev[s])
+            send(xs_.at[r, 2, top(q)], xr.at[r, top(q)], ("xr", r, q), xdev[1])
+            send(xs_.at[r, 2, bottom(q)], xr.at[r, bottom(q)], ("xr", r, q), xdev[3])
+
+    def x_pass(r, s, part, q):
+        send(xs_.at[r, s, part], xf.at[r, s // 2, part], ("xf", r, q if r else 0), xdev[s])
 
     def x_direct(r):
         for q in range(2):
-            for s, part in ((1, bottoms_of(q)), (3, tops_of(q))):
+            for s, part in ((1, bottom(q)), (3, top(q))):
                 xs_[r, s, part] = pa[r, s, part].astype(BF16)
-                x_pass(r, s, part, q, 0)
+                x_pass(r, s, part, q)
 
     def x_second(r, q):
-        for s, part, way in ((1, tops_of(q), 0), (3, bottoms_of(q), 1)):
-            arrived(xr.at[r, part], "xr", r, q, way)
+        arrived(xr.at[r, pl.ds(q * 256, 256)], "xr", r, q)
+        for s, part in ((1, top(q)), (3, bottom(q))):
             xs_[r, s, part] = (pa[r, s, part] + xr[r, part].astype(F32)).astype(BF16)
-            x_pass(r, s, part, q, 1)
-
-    def x_final(r, q):
-        for s, part, n in (
-            (1, bottoms_of(q), 0), (3, tops_of(q), 0), (1, tops_of(q), 1), (3, bottoms_of(q), 1),
-        ):
-            arrived(xf.at[s // 2, r, part], "xf", s, r, q, n)
-        part = pl.ds(q * 256, 256)
-        return pa[r, 0, part] + (xf[0, r, part].astype(F32) + xf[1, r, part].astype(F32))
+            x_pass(r, s, part, q)
 
     x_first(1)
     pa[1, 1] = project(1, 1)
@@ -450,17 +436,17 @@
     x_second(0, 0)
     x_second(0, 1)
     for q in range(2):
+        arrived(xf.at[0, 0], "xf", 1, q)
         part = pl.ds(q * 256, 256)
-        zs[part, :] = x_final(1, q).astype(BF16)
-        send(zs.at[part], zr.at[part], ("zr", q), partner)
-    for q in range(2):
-        ob[pl.ds(q * 256, 256), :] = x_final(0, q)
-    done = load(ob, out)
+        zs[part, :] = (pa[1, 0, part] + (xf[1, 0, part].astype(F32) + xf[1, 1, part].astype(F32))).astype(BF16)
+        send(zs.at[part], zr.at[part], ("zr",), partner)
+    arrived(xf.at[0], "xf", 0, 0)
+    ob[...] = pa[0, 0] + (xf[0, 0].astype(F32) + xf[0, 1].astype(F32))
+    done = load(ob, out, 6)
     all_sent()
     done.wait()
-    for q in range(2):
-        arrived(zr.at[pl.ds(q * 256, 256)], "zr", q)
-    assert (len(names), count[0]) == (RECEIVES, LOADS), (len(names), count[0])
+    arrived(zr, "zr")
+    assert len(names) == RECEIVES, len(names)
 
 
 def body(order, qh, kh, vh, og, wq, wk, wv, wo, lam, gain):

time: 54.7 us -> 52.6 us (0.962)
  Pallas kernels: 52.7 us -> 50.8 us
    pallas_call x1, Pallas kernels: 52.7 us -> 50.8 us  [body(): pl.pallas_call(kernel, out_shape=(jax.ShapeDtypeStruct((512, 128), F32),...]
where the time goes in v4:
time: 52.6 us; the launch traced here: 52.5 us
  Pallas kernels  50.8 us (97%)
  other arithmetic  1.71 us (3%)
    pallas_call x1, Pallas kernels, body(): pl.pallas_call(kernel, out_shape=(jax.ShapeDtypeStruct((512, 128), F32),...  50.8 us
    add x1, other arithmetic, body(): return parts[0] + parts[1].astype(F32)  1.71 us

profile of v4, /device:TPU:0, one launch (start us, length us, event | category | flops | bytes accessed | tf_op | source)
XLA Modules:
  0.0 52.5 jit_solution(7746969918827914957)
XLA Ops:
  0.0 50.8 %differential_attention_backward.1 = (f32[512,128]{1,0:T(8,128)}, bf16[512,128]{1,0:T(8,128)(2,1)}) custom-call(s32[32]{0:T(128)} %order_in.1, f32[2]{0:T(128)} %lam_in.1, f32[1,256]{1,0:T(1,128)} %bitcast.1, bf16[128,512]{1,0:T(8,128)(2,1)} %qh.1, bf16[128,512]{1,0:T(8,128)(2,1)} %kh.1, bf16[128,512]{1,0:T(8,128)(2,1)} %vh.1, bf16[128,512]{1,0:T(8,128)(2,1)} %og.1, ...), custom_call_target="tpu_custom_call" | custom-call | tf_op jit(solution)/shard_map/differential_attention_backward/pallas_call | solution.py:455
  50.8 1.7 %convert_add_fusion = f32[512,128]{1,0:T(8,128)} fusion(f32[512,128]{1,0:T(8,128)} %get-tuple-element.7, bf16[512,128]{1,0:T(8,128)(2,1)} %get-tuple-element.8), kind=kLoop, calls=%fused_computation | loop fusion | flops 131072 | bytes 655360 | tf_op jit(solution)/shard_map/add | solution.py:507

commit v5 on v4

--- a/solution.py
+++ b/solution.py
@@ -23,7 +23,7 @@
     return lax.dot_general(a, b, (dims, ((), ())), preferred_element_type=F32)
 
 
-RECEIVES = 42
+RECEIVES = 46
 LOADS = 7
 NT = ((1,), (1,))
 TN = ((0,), (0,))
@@ -71,15 +71,6 @@
     load(vh.at[:, half(0)], vb.at[0, 0, 0], 3)
     load(qh.at[:, half(0)], qb.at[pl.ds(0, 128)], 3)
     load(og, ogb.at[0, 0], 3)
-    for s in range(4):
-        for r in range(2):
-            block = lax.rem(lo + r, 2) * 4 + lax.rem(x + s, 4)
-            at = pl.ds(pl.multiple_of(block * 512, 512), 512)
-            load(wo.at[:, at], wob.at[r, s], 4)
-    for w, rel, group, at in (
-        (wq, 0, 0, 0), (wq, 1, 0, 256), (wk, 0, 1, 0), (wv, 0, 1, 256), (wk, 1, 2, 0), (wv, 1, 2, 256),
-    ):
-        load(w.at[:, half(rel)], wb.at[group, :, pl.ds(at, 256)], 5)
 
     def loaded(ref, n):
         pltpu.make_async_copy(ref, ref, lsem.at[n]).wait()
@@ -172,6 +163,11 @@
         term = mm(wob[r, s, rows], ogb[r, s], NT)
         gacc[rows] = term if start else gacc[rows] + term
 
+    for s in range(4):
+        for r in range(2):
+            block = lax.rem(lo + r, 2) * 4 + lax.rem(x + s, 4)
+            at = pl.ds(pl.multiple_of(block * 512, 512), 512)
+            load(wo.at[:, at], wob.at[r, s], 4)
     arrived(kb.at[1, 0, 0], "k far")
     gather_y(kb.at[1, 0, 0], kb, ("k1",), 1)
     twin(kb, 0, 1, "k1 twin")
@@ -187,6 +183,10 @@
     for s, part, to in ((3, lower, 1), (1, upper, 3)):
         send(vb.at[0, s, 0, part], vb.at[0, 2, 0, part], ("v0 relay",), ydev[to])
         twin(vb, s, 0, "v0 twin")
+    for w, rel, group, at in (
+        (wq, 0, 0, 0), (wq, 1, 0, 256), (wk, 0, 1, 0), (wv, 0, 1, 256), (wk, 1, 2, 0), (wv, 1, 2, 256),
+    ):
+        load(w.at[:, half(rel)], wb.at[group, :, pl.ds(at, 256)], 5)
     loaded(wb.at[0, pl.ds(0, 320)], 3)
     loaded(wob, 4)
     gdot(0, 0, start=True)
@@ -208,19 +208,38 @@
     arrived(kb.at[1, pl.ds(1, 3), 0], "k1")
     for s in (1, 3, 2):
         twin(kb, s, 1, "k1 twin")
+    arrived(vb.at[0, 2, 0], "v0 relay")
+    twin(vb, 2, 0, "v0 twin")
     arrived(ogb.at[1, pl.ds(0, 2)], "og", 1, False)
+    gdot(1, 1, 1)
+    gdot(1, 3, 1)
     arrived(ogb.at[1, 2], "og", 1, True)
-    for s in (1, 3, 2):
-        gdot(1, s, 1)
+    gdot(1, 2, 1)
     gs[...] = gacc[half(1)].astype(BF16)
     send(gs, gb.at[1], ("g",), far)
     for s in (1, 3, 2):
         gdot(1, s, 0)
     gb[0] = gacc[half(0)].astype(BF16)
-    arrived(vb.at[0, 2, 0], "v0 relay")
-    twin(vb, 2, 0, "v0 twin")
     for s in (3, 2):
         peak = scores(s, 0, peak)
+
+    def weigh(t, tops):
+        def step(i, sums):
+            sums = list(sums)
+            for j in range(2):
+                p = jnp.exp2(st[j, t, i] - tops[j])
+                st[j, t, i] = p
+                sums[j] = sums[j] + jnp.sum(p.reshape(16, 8, 256), axis=0)
+                pb[t, i, :, j * 256 : j * 256 + 256] = p.astype(BF16)
+            return tuple(sums)
+
+        sums = lax.fori_loop(0, 8, step, (jnp.zeros((8, 256), F32),) * 2, unroll=2)
+        return [jnp.sum(p, axis=0, keepdims=True) for p in sums]
+
+    tops0 = [jnp.max(p, axis=0, keepdims=True) for p in peak]
+    sums0 = weigh(0, tops0)
+    arrived(vb.at[0, :, 1], "v0 twin")
+    ot[...] = mm(vb[0].reshape(1024, 256), pb[0].reshape(1024, 512), TN)
     for s in (1, 3):
         arrived(vb.at[1, s, 0], "v1", "y", s)
         twin(vb, s, 1, "v1 twin", 0)
@@ -228,28 +247,17 @@
     for s in range(4):
         peak = scores(s, 1, peak)
 
+    arrived(vb.at[1, 2, 0], "v1", "y", 2)
+    twin(vb, 2, 1, "v1 twin", 1)
     tops = [jnp.max(p, axis=0, keepdims=True) for p in peak]
-
-    def weigh(i, sums):
-        sums = list(sums)
-        for t in range(2):
-            for j in range(2):
-                p = jnp.exp2(st[j, t, i] - tops[j])
-                st[j, t, i] = p
-                sums[j] = sums[j] + jnp.sum(p.reshape(16, 8, 256), axis=0)
-                pb[t, i, :, j * 256 : j * 256 + 256] = p.astype(BF16)
-        return tuple(sums)
-
-    sums = lax.fori_loop(0, 8, weigh, (jnp.zeros((8, 256), F32),) * 2)
-    inv = [1.0 / jnp.sum(p, axis=0, keepdims=True) for p in sums]
+    scales = [jnp.exp2(t0 - t1) for t0, t1 in zip(tops0, tops)]
+    sums1 = weigh(1, tops)
+    inv = [1.0 / (n * f + m) for n, f, m in zip(sums0, scales, sums1)]
 
     def values(t, s):
         return mm(vb[t, s].reshape(256, 256), pb[t, 2 * s : 2 * s + 2].reshape(256, 512), TN)
 
-    arrived(vb.at[1, 2, 0], "v1", "y", 2)
-    twin(vb, 2, 1, "v1 twin", 1)
-    arrived(vb.at[0, :, 1], "v0 twin")
-    ot[...] = mm(vb[0].reshape(1024, 256), pb[0].reshape(1024, 512), TN)
+    ot[...] = ot[...] * jnp.concatenate(scales, axis=1)
     arrived(vb.at[1, pl.ds(0, 3), 1], "v1 twin", 0)
     for s in (0, 1, 3):
         ot[...] += values(1, s)
@@ -283,8 +291,8 @@
         i = s * 2 + r
         dp = mm(vb[:, s, r].reshape(256, 256), gt[...])
         keys = kb[:, s, r].reshape(256, 256)
-        p1 = st[0, :, i].reshape(256, 256) * inv1
-        p2 = st[1, :, i].reshape(256, 256) * inv2
+        p1 = jnp.concatenate([st[0, 0, i] * (inv1 * scales[0]), st[0, 1, i] * inv1], axis=0)
+        p2 = jnp.concatenate([st[1, 0, i] * (inv2 * scales[1]), st[1, 1, i] * inv2], axis=0)
         mixed = (p1 - p2).astype(BF16)
         ds1 = (p1 * (dp - stat1)).astype(BF16)
         ds2 = (p2 * (dp - stat2)).astype(BF16)
@@ -323,7 +331,6 @@
     backward(2, 1)
     backward(2, 0)
     backward(1, 1)
-    backward(3, 1)
     def halfway(t, up, down, *key):
         send(ys.at[t, 2, :, up], yr.at[t, 0, :, up], ("halfway", t, *key), ydev[1])
         send(ys.at[t, 2, :, down], yr.at[t, 0, :, down], ("halfway", t, *key), ydev[3])
@@ -340,6 +347,7 @@
     chip_sum(1, 2, both)
     for q, (up, down) in enumerate(groups):
         halfway(1, up, down, q)
+    backward(3, 1)
     backward(1, 0)
     arrived(sibr.at[1], "sib", 1)
     straight(1, 1, right, 2)
@@ -396,30 +404,35 @@
         near = 0 if (r, s) in early else mm(wb[1, rows(r, s)], rb[1])
         return pa[r, s] + (near + mm(wb[2, rows(r, s)], rb[2]))
 
-    def top(q):
-        return pl.ds(q * 256, 128)
-
-    def bottom(q):
-        return pl.ds(q * 256 + 128, 128)
+    pieces = (2, 4)
+
+    def features(r, q):
+        return pl.ds(q * (512 // pieces[r]), 512 // pieces[r])
+
+    def top(r, q):
+        return pl.ds(q * (512 // pieces[r]), 256 // pieces[r])
+
+    def bottom(r, q):
+        return pl.ds(q * (512 // pieces[r]) + 256 // pieces[r], 256 // pieces[r])
 
     def x_first(r):
         xs_[r, 2] = project(r, 2).astype(BF16)
-        for q in range(2):
-            send(xs_.at[r, 2, top(q)], xr.at[r, top(q)], ("xr", r, q), xdev[1])
-            send(xs_.at[r, 2, bottom(q)], xr.at[r, bottom(q)], ("xr", r, q), xdev[3])
+        for q in range(pieces[r]):
+            send(xs_.at[r, 2, top(r, q)], xr.at[r, top(r, q)], ("xr", r, q), xdev[1])
+            send(xs_.at[r, 2, bottom(r, q)], xr.at[r, bottom(r, q)], ("xr", r, q), xdev[3])
 
     def x_pass(r, s, part, q):
         send(xs_.at[r, s, part], xf.at[r, s // 2, part], ("xf", r, q if r else 0), xdev[s])
 
     def x_direct(r):
-        for q in range(2):
-            for s, part in ((1, bottom(q)), (3, top(q))):
+        for q in range(pieces[r]):
+            for s, part in ((1, bottom(r, q)), (3, top(r, q))):
                 xs_[r, s, part] = pa[r, s, part].astype(BF16)
                 x_pass(r, s, part, q)
 
     def x_second(r, q):
-        arrived(xr.at[r, pl.ds(q * 256, 256)], "xr", r, q)
-        for s, part in ((1, top(q)), (3, bottom(q))):
+        arrived(xr.at[r, features(r, q)], "xr", r, q)
+        for s, part in ((1, top(r, q)), (3, bottom(r, q))):
             xs_[r, s, part] = (pa[r, s, part] + xr[r, part].astype(F32)).astype(BF16)
             x_pass(r, s, part, q)
 
@@ -430,14 +443,14 @@
     x_first(0)
     for r, s in ((0, 1), (0, 3), (1, 0), (0, 0)):
         pa[r, s] = project(r, s)
-    x_second(1, 0)
-    x_second(1, 1)
+    for q in range(pieces[1]):
+        x_second(1, q)
     x_direct(0)
-    x_second(0, 0)
-    x_second(0, 1)
-    for q in range(2):
-        arrived(xf.at[0, 0], "xf", 1, q)
-        part = pl.ds(q * 256, 256)
+    for q in range(pieces[0]):
+        x_second(0, q)
+    for q in range(pieces[1]):
+        part = features(1, q)
+        arrived(xf.at[1, :, part], "xf", 1, q)
         zs[part, :] = (pa[1, 0, part] + (xf[1, 0, part].astype(F32) + xf[1, 1, part].astype(F32))).astype(BF16)
         send(zs.at[part], zr.at[part], ("zr",), partner)
     arrived(xf.at[0], "xf", 0, 0)

time: 52.6 us -> 52.4 us (level)
  no operation moved by 1% of the time
where the time goes in v5:
time: 52.4 us; the launch traced here: 52.3 us
  Pallas kernels  50.5 us (96%)
  other arithmetic  1.71 us (3%)
    pallas_call x1, Pallas kernels, body(): pl.pallas_call(kernel, out_shape=(jax.ShapeDtypeStruct((512, 128), F32),...  50.5 us
    add x1, other arithmetic, body(): return parts[0] + parts[1].astype(F32)  1.71 us

profile of v5, /device:TPU:0, one launch (start us, length us, event | category | flops | bytes accessed | tf_op | source)
XLA Modules:
  0.0 52.3 jit_solution(14230709525220567899)
XLA Ops:
  0.0 50.5 %differential_attention_backward.1 = (f32[512,128]{1,0:T(8,128)}, bf16[512,128]{1,0:T(8,128)(2,1)}) custom-call(s32[32]{0:T(128)} %order_in.1, f32[2]{0:T(128)} %lam_in.1, f32[1,256]{1,0:T(1,128)} %bitcast.1, bf16[128,512]{1,0:T(8,128)(2,1)} %qh.1, bf16[128,512]{1,0:T(8,128)(2,1)} %kh.1, bf16[128,512]{1,0:T(8,128)(2,1)} %vh.1, bf16[128,512]{1,0:T(8,128)(2,1)} %og.1, ...), custom_call_target="tpu_custom_call" | custom-call | tf_op jit(solution)/shard_map/differential_attention_backward/pallas_call | solution.py:468
  50.5 1.7 %convert_add_fusion = f32[512,128]{1,0:T(8,128)} fusion(f32[512,128]{1,0:T(8,128)} %get-tuple-element.7, bf16[512,128]{1,0:T(8,128)(2,1)} %get-tuple-element.8), kind=kLoop, calls=%fused_computation | loop fusion | flops 131072 | bytes 655360 | tf_op jit(solution)/shard_map/add | solution.py:520

commit v6 on v5

--- a/solution.py
+++ b/solution.py
@@ -23,7 +23,7 @@
     return lax.dot_general(a, b, (dims, ((), ())), preferred_element_type=F32)
 
 
-RECEIVES = 46
+RECEIVES = 48
 LOADS = 7
 NT = ((1,), (1,))
 TN = ((0,), (0,))
@@ -331,22 +331,25 @@
     backward(2, 1)
     backward(2, 0)
     backward(1, 1)
-    def halfway(t, up, down, *key):
-        send(ys.at[t, 2, :, up], yr.at[t, 0, :, up], ("halfway", t, *key), ydev[1])
-        send(ys.at[t, 2, :, down], yr.at[t, 0, :, down], ("halfway", t, *key), ydev[3])
-
-    def second_hop(t, up, down, n):
+    def halfway(t, up, down, *key, rows=pl.ds(0, 128)):
+        send(ys.at[t, 2, rows, up], yr.at[t, 0, rows, up], ("halfway", t, *key), ydev[1])
+        send(ys.at[t, 2, rows, down], yr.at[t, 0, rows, down], ("halfway", t, *key), ydev[3])
+
+    def second_hop(t, up, down, n, rows=pl.ds(0, 128)):
         for s, cols in ((1, up), (3, down)):
-            ys[t, s, :, cols] = (total(t, s, cols) + yr[t, 0, :, cols].astype(F32)).astype(BF16)
-            pass_on(t, s, cols, n)
+            here = own[t, s, rows, cols] + sibr[s, t, rows, cols].astype(F32)
+            ys[t, s, rows, cols] = (here + yr[t, 0, rows, cols].astype(F32)).astype(BF16)
+            send(ys.at[t, s, rows, cols], yr.at[t, s, rows, cols], ("yr", t, n), ydev[s])
 
     groups = [(pl.ds(q * 128, 128), pl.ds(256 + q * 128, 128)) for q in range(2)]
     a_group = yr.at[1, 0, :, left]
 
     arrived(sibr.at[2], "sib", 2)
     chip_sum(1, 2, both)
+    row_halves = [pl.ds(0, 64), pl.ds(64, 64)]
     for q, (up, down) in enumerate(groups):
-        halfway(1, up, down, q)
+        for h in range(2):
+            halfway(1, up, down, q, h, rows=row_halves[h])
     backward(3, 1)
     backward(1, 0)
     arrived(sibr.at[1], "sib", 1)
@@ -363,8 +366,9 @@
         dqs[j * 128 : j * 128 + 128] = (dq[j, :, 128:256] * sign).astype(BF16)
     send(dqs, rb.at[0, pl.ds(256, 256)], ("dq",), far)
     for q, (up, down) in enumerate(groups):
-        arrived(a_group, "halfway", 1, q)
-        second_hop(1, up, down, q)
+        for h in range(2):
+            arrived(yr.at[1, 0, row_halves[h], left], "halfway", 1, q, h)
+            second_hop(1, up, down, q, row_halves[h])
     straight(0, 1, right, 0)
     straight(0, 3, left, 0)
     arrived(sibr.at[0], "sib", 0)

time: 52.4 us -> 52.4 us (level)
  no operation moved by 1% of the time
where the time goes in v6:
time: 52.4 us; the launch traced here: 52.3 us
  Pallas kernels  50.6 us (97%)
  other arithmetic  1.71 us (3%)
    pallas_call x1, Pallas kernels, body(): pl.pallas_call(kernel, out_shape=(jax.ShapeDtypeStruct((512, 128), F32),...  50.6 us
    add x1, other arithmetic, body(): return parts[0] + parts[1].astype(F32)  1.71 us

profile of v6, /device:TPU:0, one launch (start us, length us, event | category | flops | bytes accessed | tf_op | source)
XLA Modules:
  0.0 52.3 jit_solution(2004640016288028945)
XLA Ops:
  0.0 50.6 %differential_attention_backward.1 = (f32[512,128]{1,0:T(8,128)}, bf16[512,128]{1,0:T(8,128)(2,1)}) custom-call(s32[32]{0:T(128)} %order_in.1, f32[2]{0:T(128)} %lam_in.1, f32[1,256]{1,0:T(1,128)} %bitcast.1, bf16[128,512]{1,0:T(8,128)(2,1)} %qh.1, bf16[128,512]{1,0:T(8,128)(2,1)} %kh.1, bf16[128,512]{1,0:T(8,128)(2,1)} %vh.1, bf16[128,512]{1,0:T(8,128)(2,1)} %og.1, ...), custom_call_target="tpu_custom_call" | custom-call | tf_op jit(solution)/shard_map/differential_attention_backward/pallas_call | solution.py:472
  50.6 1.7 %convert_add_fusion = f32[512,128]{1,0:T(8,128)} fusion(f32[512,128]{1,0:T(8,128)} %get-tuple-element.7, bf16[512,128]{1,0:T(8,128)(2,1)} %get-tuple-element.8), kind=kLoop, calls=%fused_computation | loop fusion | flops 131072 | bytes 655360 | tf_op jit(solution)/shard_map/add | solution.py:524
